TPU v7x, 256 devices: a whole 4x4x8 slice. The times are simulated.
256 devices in a mesh: tm: 8 (over x, core), seq: 32 (over y, z).
Axes of the slice: x: 4, y: 4, z: 8, core: 2. Of those that a mesh axis runs over, the one named last changes fastest.
Arguments:
- rgb_feat: bfloat16 [8, 16384, 1024], P('tm', 'seq'), may hold values from -60 to 60
- rgb_grad_out: bfloat16 [8, 16384, 1024], P('tm', 'seq'), may hold values from -6 to 6
- pose_feat: bfloat16 [8, 4096, 1024], P('tm', 'seq'), may hold values from -12 to 12
- pose_grad_out: bfloat16 [8, 4096, 1024], P('tm', 'seq'), may hold values from -6 to 6
- logit_scale: float32 [8], replicated, may hold values from 0.5 to 2.5
- pairs: int32 [8, 160], P('tm', 'seq'), may hold values from -1 to 127, as said below
Outputs:
- rgb_grad: bfloat16 [8, 16384, 1024], P('tm', 'seq')
- pose_grad: bfloat16 [8, 4096, 1024], P('tm', 'seq')
- scale_grad: float32 [8], replicated
Inputs may be any that keep to these rules, and one draw needn't show every extreme that they name: `pairs`: each entry is -1 or rgb_tile * 32 + pose_tile with rgb_tile below 4, naming one of the device's own RGB tiles and the pose tile of seq index pose_tile of the same time group. Live entries come first and never repeat within a device's list; in every time group some device has all 5 entries live.
All inputs are finite; a program needn't handle non-finite values.
Results may differ from a plain program's by a relative error of at most 0.023.
Values may be sent and summed in bfloat16 or wider, within the bound.
A program may use at most 128 MiB of HBM per device.

v0:
```python
import math

import jax
import jax.numpy as jnp
from jax import lax
from jax.sharding import PartitionSpec as P

NEG = -1e30


def merged(part, axis, combine):
    gathered = jax.tree.map(lambda a: lax.all_gather(a, axis), part)

    def take(source):
        return jax.tree.map(lambda a: lax.dynamic_index_in_dim(a, source, 0, False), gathered)

    return lax.fori_loop(
        1, lax.axis_size(axis), lambda source, state: combine(state, take(source)), take(0)
    )


def split_heads(values, head_count):
    return values.reshape(values.shape[:-1] + (head_count, values.shape[-1] // head_count))


def product(pattern, former, latter):
    return jnp.einsum(pattern, former, latter, preferred_element_type=jnp.float32)


def group_max(hot_table, values):
    return jnp.max(jnp.where(hot_table[:, :, None, None], values[:, None], NEG), axis=0)


def group_sum(hot_table, values):
    return jnp.einsum(
        "pt,p...->t...", hot_table.astype(jnp.float32), values, precision=lax.Precision.HIGHEST
    )


def score_tiles(rgb_blocks, pose_blocks, pose_cots, logit_scale):
    head_count = logit_scale.shape[0]
    split_rgb = split_heads(rgb_blocks, head_count)
    head_dim = rgb_blocks.shape[-1] // head_count
    raw_dot = product(
        "pihe,pjhe->phij", split_rgb, split_heads(pose_blocks, head_count)
    ) / math.sqrt(head_dim)
    scores = raw_dot * logit_scale[None, :, None, None]
    pose_dot = product("pihe,pjhe->phij", split_rgb, split_heads(pose_cots, head_count))
    return (raw_dot, scores, pose_dot)


def merge_stats(former, latter):
    highest = jnp.maximum(former[0], latter[0])
    former_scale = jnp.exp(former[0] - highest)
    latter_scale = jnp.exp(latter[0] - highest)
    return (
        highest,
        former[1] * former_scale + latter[1] * latter_scale,
        former[2] * former_scale + latter[2] * latter_scale,
    )


def local(rgb_feat, rgb_grad_out, pose_feat, pose_grad_out, logit_scale, pairs):
    seq_count = lax.axis_size("seq")
    tile_rows = pose_feat.shape[1]
    feat_width = pose_feat.shape[2]
    head_count = logit_scale.shape[0]
    head_dim = feat_width // head_count
    own_rows = rgb_feat[0]
    block_count = own_rows.shape[0] // tile_rows
    stacked = jnp.stack([pose_feat[0], pose_grad_out[0]])
    gathered = lax.all_gather(stacked, "seq", axis=1, tiled=True)
    pose_all = gathered[0].reshape(seq_count, tile_rows, feat_width)
    pose_cot_all = gathered[1].reshape(seq_count, tile_rows, feat_width)
    pair_codes = pairs[0]
    is_live = pair_codes >= 0
    clamped = jnp.maximum(pair_codes, 0)
    rgb_index = clamped // seq_count
    pose_index = clamped % seq_count
    rgb_blocks = own_rows.reshape(block_count, tile_rows, feat_width)[rgb_index]
    rgb_cots = rgb_grad_out[0].reshape(block_count, tile_rows, feat_width)[rgb_index]
    pose_blocks = pose_all[pose_index]
    pose_cots = pose_cot_all[pose_index]
    rgb_hot = (rgb_index[:, None] == jnp.arange(block_count)[None, :]) & is_live[:, None]
    pose_hot = (pose_index[:, None] == jnp.arange(seq_count)[None, :]) & is_live[:, None]
    live_four = is_live[:, None, None, None]
    raw_dot, scores, pose_dot = score_tiles(rgb_blocks, pose_blocks, pose_cots, logit_scale)
    row_max = jnp.where(is_live[:, None, None], jnp.max(scores, axis=3), NEG)
    pair_max = group_max(rgb_hot, row_max)[rgb_index]
    row_weights = jnp.where(live_four, jnp.exp(scores - pair_max[..., None]), 0.0)
    rgb_den = jnp.maximum(group_sum(rgb_hot, jnp.sum(row_weights, axis=3)), 1.0)[rgb_index]
    col_max = jnp.where(is_live[:, None, None], jnp.max(scores, axis=2), NEG)
    part_max = group_max(pose_hot, col_max)
    col_weights = jnp.where(live_four, jnp.exp(scores - part_max[pose_index][:, :, None, :]), 0.0)
    part_sum = group_sum(pose_hot, jnp.sum(col_weights, axis=2))
    part_dot = group_sum(pose_hot, jnp.sum(col_weights * pose_dot, axis=2))
    pose_max, pose_total, pose_inner = merged((part_max, part_sum, part_dot), "seq", merge_stats)
    pose_den = jnp.maximum(pose_total, 1.0)
    pose_gam = pose_inner / pose_den
    kept = lax.optimization_barrier((rgb_blocks, pose_blocks, pose_cots))
    raw_dot, scores, pose_dot = score_tiles(kept[0], kept[1], kept[2], logit_scale)
    rgb_prob = jnp.where(live_four, jnp.exp(scores - pair_max[..., None]) / rgb_den[..., None], 0.0)
    pose_prob = jnp.where(
        live_four,
        jnp.exp(scores - pose_max[pose_index][:, :, None, :]) / pose_den[pose_index][:, :, None, :],
        0.0,
    )
    grad_p = product(
        "pihe,pjhe->phij", split_heads(rgb_cots, head_count), split_heads(pose_blocks, head_count)
    )
    row_delta = group_sum(rgb_hot, jnp.sum(rgb_prob * grad_p, axis=3))[rgb_index]
    dscore = rgb_prob * (grad_p - row_delta[..., None]) + pose_prob * (
        pose_dot - pose_gam[pose_index][:, :, None, :]
    )
    dscore_low = dscore.astype(jnp.bfloat16)
    rgb_low = rgb_prob.astype(jnp.bfloat16)
    pose_low = pose_prob.astype(jnp.bfloat16)
    head_scale = (logit_scale / math.sqrt(head_dim))[None, None, :, None]
    rgb_part = product(
        "phij,pjhe->pihe", pose_low, split_heads(pose_cots, head_count)
    ) + head_scale * product("phij,pjhe->pihe", dscore_low, split_heads(pose_blocks, head_count))
    pose_part = product(
        "phij,pihe->pjhe", rgb_low, split_heads(rgb_cots, head_count)
    ) + head_scale * product("phij,pihe->pjhe", dscore_low, split_heads(rgb_blocks, head_count))
    rgb_rows = group_sum(rgb_hot, rgb_part).reshape(block_count * tile_rows, feat_width)
    pose_terms = group_sum(pose_hot, pose_part).reshape(seq_count * tile_rows, feat_width)
    scale_term = jnp.sum(dscore * raw_dot, axis=(0, 2, 3))
    pose_total_grad = lax.psum_scatter(
        pose_terms.astype(jnp.bfloat16), "seq", scatter_dimension=0, tiled=True
    )
    scale_grad = lax.psum(scale_term, ("tm", "seq"))
    return (rgb_rows.astype(jnp.bfloat16)[None], pose_total_grad[None], scale_grad)


def solution(mesh):
    return jax.shard_map(
        local,
        mesh=mesh,
        in_specs=(
            P("tm", "seq", None),
            P("tm", "seq", None),
            P("tm", "seq", None),
            P("tm", "seq", None),
            P(),
            P("tm", "seq"),
        ),
        out_specs=(P("tm", "seq", None), P("tm", "seq", None), P()),
        check_vma=False,
    )
```

profile of v0, /device:TPU:2, one launch (start us, length us, event | category | flops | bytes accessed | tf_op | source)
XLA Modules:
  0.0 794.5 jit_solution(12326896760015958119)
XLA Ops:
  12.3 142.5 %all-gather.8.cloned.1.call-done = bf16[2,4096,1024]{2,1,0:T(8,128)(2,1)} async-done(((bf16[2,128,1024]{2,1,0:T(8,128)(2,1)}), bf16[2,4096,1024]{2,1,0:T(8,128)(2,1)}) %all-gather.8.cloned.1.call-update) | async-done | bytes 16777232 | tf_op jit(solution)/shard_map/all_gather | solution.py:72
  154.8 11.6 %fusion.41 = (bf16[1,4096,1024]{2,1,0:T(8,128)(2,1)}, bf16[1,4096,1024]{2,1,0:T(8,128)(2,1)}) fusion(bf16[2,4096,1024]{2,1,0:T(8,128)(2,1)} %all-gather.8.cloned.1.call-done), kind=kLoop, calls=%fused_computation.89 | loop fusion | bytes 33554432 | tf_op jit(solution)/shard_map/slice | solution.py:73
  166.4 5.2 gather_fusion.2
  171.6 2.5 copy.128
  174.0 3.9 multiply_reduce_fusion.3
  179.5 3.1 select_reduce_fusion
  183.7 5.3 gather_fusion
  191.4 4.6 multiply_reduce_fusion.2
  203.5 2.6 copy.124
  208.2 2.5 fusion.42
  210.7 2.5 multiply_reduce_fusion.1
  214.0 4.7 fusion.12
  218.7 44.0 %all-gather.12.cloned.1.call-done = f32[1024,8,128]{2,0,1:T(8,128)} async-done(((f32[32,8,128]{2,0,1:T(8,128)}), f32[1024,8,128]{2,0,1:T(8,128)}) %all-gather.12.cloned.1.call-update) | async-done | bytes 4194320 | tf_op jit(solution)/shard_map/all_gather | solution.py:12
  263.7 80.7 %all-gather.14.cloned.1.call-done = f32[1024,8,128]{2,0,1:T(8,128)} async-done(((f32[32,8,128]{2,0,1:T(8,128)}), f32[1024,8,128]{2,0,1:T(8,128)}) %all-gather.14.cloned.1.call-update) | async-done | bytes 4194320 | tf_op jit(solution)/shard_map/all_gather | solution.py:12
  345.4 81.1 %all-gather.10.cloned.1.call-done = f32[1024,8,128]{2,1,0:T(8,128)} async-done(((f32[32,8,128]{2,1,0:T(8,128)}), f32[1024,8,128]{2,1,0:T(8,128)}) %all-gather.10.cloned.1.call-update) | async-done | bytes 4194320 | tf_op jit(solution)/shard_map/all_gather | solution.py:12
  427.4 96.1 %while.19 = (s32[]{:T(128)}, f32[32,8,128]{2,1,0:T(8,128)S(1)}, f32[32,8,128]{2,1,0:T(8,128)S(1)}, f32[32,8,128]{2,1,0:T(8,128)S(1)}, f32[32,32,8,128]{3,2,1,0:T...) while((s32[]{:T(128)}, f32[32,8,128]{2,1,0:T(8,128)S(1)}, ...), condition=%wide.region_5.6_spmd, body=%wide.region_4.5_spmd.sunk | while | flops 360453 | bytes 2359451 | solution.py:17
  525.2 5.2 multiply_reduce_fusion
  531.5 11.2 %convolution_convert_fusion = bf16[32,128,8,128]{3,0,2,1:T(8,128)(2,1)} fusion(f32[5,128,8,128]{3,1,2,0:T(8,128)S(1)} %add_bitcast_fusion, s32[5]{0:T(128)S(1)} %get-tuple-element.252, pred[5]{0:T(512)(128)(4,1)S(1)} %compare_bitcast_fusion), kind=kOutput, calls=%fused_computation.24 | convolution fusion | flops 255852864 | bytes 11010073 | tf_op jit(solution)/shard_map/pt,p...->t.../dot_general | solution.py:35
  542.6 9.8 %copy.165 = bf16[32,128,8,128]{3,2,1,0:T(8,128)(2,1)} copy(bf16[32,128,8,128]{3,0,2,1:T(8,128)(2,1)} %convolution_convert_fusion) | data formatting | bytes 16777216 | tf_op jit(solution)/shard_map/convert_element_type | solution.py:129
  552.5 8.8 %copy.217 = bf16[512,8,8,128]{3,1,2,0:T(8,128)(2,1)} copy(bf16[512,8,8,128]{3,2,1,0:T(8,128)(2,1)} %bitcast.122) | data formatting | bytes 16777216
  561.3 73.8 %psum.7 = f32[8]{0:T(128)} all-reduce(f32[8]{0:T(128)S(1)} %get-tuple-element.260), channel_id=1, replica_groups=mesh['tm'=8,'seq'=32] {'tm','seq'}, use_global_device_ids=true, to_apply=%region_12.13 | all-reduce | flops 8 | bytes 64 | tf_op jit(solution)/shard_map/psum | solution.py:131
  635.1 4.2 fusion.14
  640.4 3.9 fusion.9
  645.7 142.3 %reduce-scatter.2.cloned.1.call-done = bf16[128,1024]{1,0:T(8,128)(2,1)} async-done(((bf16[4096,1024]{1,0:T(8,128)(2,1)}), bf16[128,1024]{1,0:T(8,128)(2,1)}) %reduce-scatter.2.cloned.1.call-update) | async-done | bytes 262160 | tf_op jit(solution)/shard_map/reduce_scatter | solution.py:128
  (204 shorter events, 123.5 us)
Async XLA Ops:
  7.2 2.8 copy-start
  7.2 147.6 %all-gather.8.cloned.1.call-start = ((), (), s32[]{:S(2)}) async-start(), calls=%async_computation.1 | async-start | bytes 17301504 | tf_op jit(solution)/shard_map/all_gather | solution.py:72
  9.2 253.5 %all-gather.12.cloned.1.call-start = ((), (), s32[]{:S(2)}) async-start(), calls=%async_computation.4 | async-start | bytes 4325376 | tf_op jit(solution)/shard_map/all_gather | solution.py:12
  9.9 2.1 copy-start.12
  10.0 2.3 copy-start.13
  178.9 10.0 %copy-start.11 = (f32[32,8,128]{2,1,0:T(8,128)}, f32[32,8,128]{2,1,0:T(8,128)S(1)}, u32[]{:S(2)}) copy-start(f32[32,8,128]{2,1,0:T(8,128)S(1)} %select_reduce_fusion.1) | copy-start | bytes 393220
  183.6 160.8 %all-gather.14.cloned.1.call-start = ((), (), s32[]{:S(2)}) async-start(), calls=%async_computation.5 | async-start | bytes 4325376 | tf_op jit(solution)/shard_map/all_gather | solution.py:12
  191.4 6.5 copy-start.9
  197.0 229.4 %all-gather.10.cloned.1.call-start = ((), (), s32[]{:S(2)}) async-start(), calls=%async_computation.3 | async-start | bytes 4325376 | tf_op jit(solution)/shard_map/all_gather | solution.py:12
  197.6 590.4 %reduce-scatter.2.cloned.1.call-start = ((), (), s32[]{:S(2)}) async-start(), calls=%async_computation.2 | async-start | bytes 8650752 | tf_op jit(solution)/shard_map/reduce_scatter | solution.py:128
  203.5 2.6 copy-start.2
  208.2 2.5 copy-start.3
  208.2 2.5 copy-start.10
  210.7 2.6 copy-start.7
  525.2 5.2 copy-start.4
  525.2 5.2 copy-start.8
  530.4 1.1 copy-start.5
  635.1 4.2 copy-start.6
  640.4 147.6 %copy-start.1 = (bf16[1,512,1024]{2,1,0:T(8,128)(2,1)S(1)}, bf16[1,512,1024]{2,1,0:T(8,128)(2,1)}, u32[]{:S(2)}) copy-start(bf16[1,512,1024]{2,1,0:T(8,128)(2,1)} %param.8) | copy-start | bytes 3145732
Sparse Core Ops, SparseCore 0:
  11.2 143.5 all-gather.7
  183.7 78.8 all-gather.11
  265.3 79.0 all-gather.13
  347.4 79.0 all-gather.9
  561.4 226.5 reduce-scatter.1
where the time goes:
time: 797 us; the launch traced here: 795 us
  waiting for transfers between devices  491 us (62%)
  local copies, waits for them, and re-layouts  97 us (12%)
  blocking collectives  73.8 us (9%)
  other arithmetic  70 us (9%)
  matrix products  47.1 us (6%)
  between operations  14.1 us (2%)
    all_gather x3, waiting for transfers between devices, merged(): gathered = jax.tree.map(lambda a: lax.all_gather(a, axis), part)  206 us
    all_gather x1, waiting for transfers between devices, local(): gathered = lax.all_gather(stacked, 'seq', axis=1, tiled=True)  142 us
    reduce_scatter x1, waiting for transfers between devices, local(): lax.psum_scatter(pose_terms.astype(jnp.bfloat16), 'seq', scatter_dimensio...  142 us
    psum x1, blocking collectives, local(): scale_grad = lax.psum(scale_term, ('tm', 'seq'))  73.8 us
    dynamic_slice x34, local copies, waits for them, and re-layouts, take(): lax.dynamic_index_in_dim(a, source, 0, False)  33.7 us
    add x31, other arithmetic, merge_stats(): former[2] * former_scale + latter[2] * latter_scale  32.1 us
    add x31, other arithmetic, merge_stats(): former[1] * former_scale + latter[1] * latter_scale  31.7 us
    dot_general x9, matrix products, product(): jnp.einsum(pattern, former, latter, preferred_element_type=jnp.float32)  29.8 us
  transfers between devices with their start and end apart: 5, of which 5 were waited for; matrix products, arithmetic and copies ran while one was open for 6% of the time, Pallas kernels for 0%

commit v1 on v0

v1 whole, which is shorter than its diff:
```python
import functools
import math

import jax
import jax.numpy as jnp
from jax import lax
from jax.experimental import pallas as pl
from jax.experimental.pallas import tpu as pltpu
from jax.sharding import PartitionSpec as P

NEG = -1e30
NY = 4
NZ = 8
NT = 8
TILE = 128
HD = 128
SLOTS = 5
WIDE = 256
VMEM_LIMIT = 56 * 1024 * 1024
MESH = pl.DeviceIdType.MESH
ANY = pl.BlockSpec(memory_space=pl.ANY)
VM = pl.BlockSpec(memory_space=pltpu.VMEM)
SM = pl.BlockSpec(memory_space=pltpu.SMEM)


def place():
    me = lax.axis_index("seq")
    return me // NZ, me % NZ


def remote(src, dst, send_sem, recv_sem, y, z):
    return pltpu.make_async_remote_copy(
        src_ref=src,
        dst_ref=dst,
        send_sem=send_sem,
        recv_sem=recv_sem,
        device_id={"seq": y * NZ + z},
        device_id_type=MESH,
    )


def remote_tm(src, dst, send_sem, recv_sem, t):
    return pltpu.make_async_remote_copy(
        src_ref=src,
        dst_ref=dst,
        send_sem=send_sem,
        recv_sem=recv_sem,
        device_id={"tm": t},
        device_id_type=MESH,
    )


def greet(seqs, tms=()):
    barrier = pltpu.get_barrier_semaphore()
    for y, z in seqs:
        pl.semaphore_signal(
            barrier, inc=1, device_id={"seq": y * NZ + z}, device_id_type=MESH
        )
    for t in tms:
        pl.semaphore_signal(barrier, inc=1, device_id={"tm": t}, device_id_type=MESH)
    pl.semaphore_wait(barrier, len(seqs) + len(tms))


def columns(y):
    return pl.ds(pl.multiple_of(y * WIDE, WIDE), WIDE)


def gather_kernel(
    rgb_ref, cot_ref, pf_ref, pc_ref, pairs_ref,
    rgbx, cotx, pose, pairs_x,
    local_sem, y_send, y_recv, z_send, z_recv,
):
    y, z = place()
    greet(
        [((y + k) % NY, z) for k in (1, 2, 3)]
        + [(y, (z + 1) % NZ), (y, (z + NZ - 1) % NZ)]
    )

    def y_copies(k):
        to = (y + k) % NY
        cols = columns(to)
        parts = (
            (pf_ref.at[:, cols], pose.at[z * NY + y, 0]),
            (pc_ref.at[:, cols], pose.at[z * NY + y, 1]),
            (pairs_ref, pairs_x.at[y]),
            (rgb_ref.at[:, :, cols], rgbx.at[pl.ds(y * 4, 4)]),
            (cot_ref.at[:, :, cols], cotx.at[pl.ds(y * 4, 4)]),
        )
        if k == 0:
            return [
                pltpu.make_async_copy(src, dst, local_sem.at[i])
                for i, (src, dst) in enumerate(parts)
            ]
        return [
            remote(src, dst, y_send.at[k - 1, i], y_recv.at[k - 1, i], to, z)
            for i, (src, dst) in enumerate(parts)
        ]

    own = y_copies(0)
    across = {k: y_copies(k) for k in (1, 2, 3)}
    own[0].start()
    own[1].start()
    for i in range(3):
        for k in (1, 2, 3):
            across[k][i].start()
    own[2].start()

    def hop(side, step, c):
        block = (z + NZ - step) % NZ if side == 0 else (z + step) % NZ
        to = (z + 1) % NZ if side == 0 else (z + NZ - 1) % NZ
        ref = pose.at[block * NY + (y + NY - c) % NY]
        return remote(ref, ref, z_send.at[side, step, c], z_recv.at[side, step, c], y, to)

    def used(side, step, c):
        return step < 3 or (c < 2) == (side == 0)

    sent = []
    for step in range(4):
        for c in range(NY):
            if step == 0:
                if c == 0:
                    own[0].wait()
                    own[1].wait()
                else:
                    across[c][0].wait_recv()
                    across[c][1].wait_recv()
            for side in range(2):
                if step > 0:
                    hop(side, step - 1, c).wait_recv()
                if used(side, step, c):
                    copy = hop(side, step, c)
                    copy.start()
                    sent.append(copy)
            if step == 0 and c == 0:
                for i in (3, 4):
                    for k in (1, 2, 3):
                        across[k][i].start()
                    own[i].start()
    for c in range(NY):
        for side in range(2):
            if used(side, 3, c):
                hop(side, 3, c).wait_recv()
    for k in (1, 2, 3):
        for i in (2, 3, 4):
            across[k][i].wait_recv()
    for i in (2, 3, 4):
        own[i].wait()
    for k in (1, 2, 3):
        for i in range(5):
            across[k][i].wait_send()
    for copy in sent:
        copy.wait_send()


def gather(rgb, cot, pf, pc, pairs):
    return pl.pallas_call(
        gather_kernel,
        out_shape=(
            jax.ShapeDtypeStruct((16, TILE, WIDE), jnp.bfloat16),
            jax.ShapeDtypeStruct((16, TILE, WIDE), jnp.bfloat16),
            jax.ShapeDtypeStruct((NY * NZ, 2, TILE, WIDE), jnp.bfloat16),
            jax.ShapeDtypeStruct((NY, 1, SLOTS), jnp.int32),
        ),
        in_specs=[ANY] * 5,
        out_specs=(ANY,) * 4,
        scratch_shapes=[
            pltpu.SemaphoreType.DMA((5,)),
            pltpu.SemaphoreType.DMA((3, 5)),
            pltpu.SemaphoreType.DMA((3, 5)),
            pltpu.SemaphoreType.DMA((2, 4, 4)),
            pltpu.SemaphoreType.DMA((2, 4, 4)),
        ],
        compiler_params=pltpu.CompilerParams(
            collective_id=0, has_side_effects=True, vmem_limit_bytes=VMEM_LIMIT
        ),
    )(rgb, cot, pf, pc, pairs)


def dot_t(a, b):
    return lax.dot_general(a, b, (((1,), (1,)), ((), ())), preferred_element_type=jnp.float32)


def merge_into(ref, index, h, high, total, inner):
    old = ref[index, pl.ds(h, 1), :]
    top = jnp.maximum(old, high)
    keep = jnp.exp(old - top)
    add = jnp.exp(high - top)
    ref[index, pl.ds(h, 1), :] = top
    ref[index, pl.ds(2 + h, 1), :] = ref[index, pl.ds(2 + h, 1), :] * keep + total * add
    ref[index, pl.ds(4 + h, 1), :] = ref[index, pl.ds(4 + h, 1), :] * keep + inner * add


def pair_index(pairs, n):
    r = n // SLOTS
    code = pairs[r, 0, n % SLOTS]
    kept = jnp.maximum(code, 0)
    tile = kept % (NY * NZ)
    return code >= 0, r * 4 + kept // (NY * NZ), (tile % NZ) * NY + tile // NZ


def stats_kernel(pairs, scale, rgbx, cotx, pose, st, rs):
    row = lax.broadcasted_iota(jnp.int32, (1, 8, HD), 1)
    blank = jnp.where(row < 2, NEG, 0.0)
    st[...] = jnp.broadcast_to(blank, st.shape)
    rs[...] = jnp.broadcast_to(blank, rs.shape)

    def body(n, carry):
        live, ri, pi = pair_index(pairs, n)

        @pl.when(live)
        def _():
            for h in range(2):
                cols = pl.ds(h * HD, HD)
                factor = scale[h] / math.sqrt(HD)
                q = rgbx[ri, :, cols]
                g = cotx[ri, :, cols]
                both = pose[pi, :, :, cols].reshape(2 * TILE, HD)
                pf = pose[pi, 0, :, cols]
                dots = dot_t(q, both)
                score = dots[:, :TILE] * factor
                high = jnp.max(score, axis=0, keepdims=True)
                w = jnp.exp(score - high)
                merge_into(
                    st, pi, h, high,
                    jnp.sum(w, axis=0, keepdims=True),
                    jnp.sum(w * dots[:, TILE:], axis=0, keepdims=True),
                )
                score = dot_t(pf, q) * factor
                grad = dot_t(pf, g)
                high = jnp.max(score, axis=0, keepdims=True)
                w = jnp.exp(score - high)
                merge_into(
                    rs, ri, h, high,
                    jnp.sum(w, axis=0, keepdims=True),
                    jnp.sum(w * grad, axis=0, keepdims=True),
                )

        return carry

    lax.fori_loop(0, NY * SLOTS, body, 0)


def stats(pairs, scale, rgbx, cotx, pose):
    return pl.pallas_call(
        stats_kernel,
        out_shape=(
            jax.ShapeDtypeStruct((NY * NZ, 8, HD), jnp.float32),
            jax.ShapeDtypeStruct((16, 8, HD), jnp.float32),
        ),
        in_specs=[SM, SM, VM, VM, VM],
        out_specs=(VM, VM),
        compiler_params=pltpu.CompilerParams(vmem_limit_bytes=VMEM_LIMIT),
    )(pairs, scale, rgbx, cotx, pose)


def exchange_kernel(st, fin, got, send1, recv1, send2, recv2):
    y, z = place()
    greet([(y, (z + k) % NZ) for k in range(1, NZ)])

    def first(k):
        to = (z + k) % NZ
        return remote(
            st.at[pl.ds(to * NY, NY)], got.at[z], send1.at[k - 1], recv1.at[k - 1], y, to
        )

    def second(k):
        to = (z + k) % NZ
        ref = fin.at[pl.ds(z * NY, NY)]
        return remote(ref, ref, send2.at[k - 1], recv2.at[k - 1], y, to)

    for k in range(1, NZ):
        first(k).start()
    got[z] = st[pl.ds(z * NY, NY)]
    for k in range(1, NZ):
        first(k).wait_recv()
    top = got[0, :, 0:2, :]
    for k in range(1, NZ):
        top = jnp.maximum(top, got[k, :, 0:2, :])
    total = jnp.zeros_like(top)
    inner = jnp.zeros_like(top)
    for k in range(NZ):
        keep = jnp.exp(got[k, :, 0:2, :] - top)
        total += got[k, :, 2:4, :] * keep
        inner += got[k, :, 4:6, :] * keep
    inverse = 1.0 / jnp.maximum(total, 1.0)
    mine = pl.ds(z * NY, NY)
    fin[mine, 0:2, :] = top
    fin[mine, 2:4, :] = inverse
    fin[mine, 4:6, :] = inner * inverse
    fin[mine, 6:8, :] = jnp.zeros_like(top)
    for k in range(1, NZ):
        second(k).start()
    for k in range(1, NZ):
        second(k).wait_recv()
    for k in range(1, NZ):
        first(k).wait_send()
        second(k).wait_send()


def exchange(st):
    return pl.pallas_call(
        exchange_kernel,
        out_shape=jax.ShapeDtypeStruct((NY * NZ, 8, HD), jnp.float32),
        in_specs=[VM],
        out_specs=VM,
        scratch_shapes=[pltpu.VMEM((NZ, NY, 8, HD), jnp.float32)]
        + [pltpu.SemaphoreType.DMA((NZ - 1,))] * 4,
        compiler_params=pltpu.CompilerParams(
            collective_id=1, has_side_effects=True, vmem_limit_bytes=VMEM_LIMIT
        ),
    )(st)


def backward_kernel(
    pairs, scale, rgbx, cotx, pose, rs, fin, rgb_out, pose_out, scale_out, racc, pacc, sacc
):
    racc[...] = jnp.zeros_like(racc)
    pacc[...] = jnp.zeros_like(pacc)
    sacc[...] = jnp.zeros_like(sacc)

    def body(n, carry):
        live, ri, pi = pair_index(pairs, n)

        @pl.when(live)
        def _():
            rows = rs[ri]
            inverse = 1.0 / jnp.maximum(rows[2:4], 1.0)
            rows = jnp.concatenate(
                [rows[0:2], inverse, rows[4:6] * inverse, jnp.zeros((2, HD), jnp.float32)], axis=0
            )
            rows = jnp.transpose(rows)
            for h in range(2):
                cols = pl.ds(h * HD, HD)
                factor = scale[h] / math.sqrt(HD)
                q = rgbx[ri, :, cols]
                g = cotx[ri, :, cols]
                both = pose[pi, :, :, cols].reshape(2 * TILE, HD)
                pf = pose[pi, 0, :, cols]
                pc = pose[pi, 1, :, cols]
                dots = dot_t(q, both)
                raw = dots[:, :TILE]
                score = raw * factor
                grad = dot_t(g, pf)
                pr = jnp.exp(score - rows[:, h:h + 1]) * rows[:, 2 + h:3 + h]
                pp = jnp.exp(score - fin[pi, pl.ds(h, 1), :]) * fin[pi, pl.ds(2 + h, 1), :]
                ds = pr * (grad - rows[:, 4 + h:5 + h]) + pp * (
                    dots[:, TILE:] - fin[pi, pl.ds(4 + h, 1), :]
                )
                sacc[h] += jnp.sum((ds * raw).reshape(TILE // 8, 8, HD), axis=0)
                ds_low = ds.astype(jnp.bfloat16)
                pr_low = pr.astype(jnp.bfloat16)
                pp_low = pp.astype(jnp.bfloat16)
                racc[ri, :, cols] += jnp.dot(
                    pp_low, pc, preferred_element_type=jnp.float32
                ) + factor * jnp.dot(ds_low, pf, preferred_element_type=jnp.float32)
                turned = (((0,), (0,)), ((), ()))
                pacc[pi, :, cols] += lax.dot_general(
                    pr_low, g, turned, preferred_element_type=jnp.float32
                ) + factor * lax.dot_general(
                    ds_low, q, turned, preferred_element_type=jnp.float32
                )

        return carry

    lax.fori_loop(0, NY * SLOTS, body, 0)
    rgb_out[...] = racc[...].astype(jnp.bfloat16)
    pose_out[...] = pacc[...].astype(jnp.bfloat16)
    for h in range(2):
        part = jnp.sum(sacc[h], axis=0, keepdims=True)
        part = jnp.sum(part, axis=1, keepdims=True) / math.sqrt(HD)
        scale_out[pl.ds(h, 1), :] = jnp.broadcast_to(part, (1, HD))
    scale_out[pl.ds(2, 6), :] = jnp.zeros((6, HD), jnp.float32)


def backward(pairs, scale, rgbx, cotx, pose, rs, fin):
    return pl.pallas_call(
        backward_kernel,
        out_shape=(
            jax.ShapeDtypeStruct((16, TILE, WIDE), jnp.bfloat16),
            jax.ShapeDtypeStruct((NY * NZ, TILE, WIDE), jnp.bfloat16),
            jax.ShapeDtypeStruct((8, HD), jnp.float32),
        ),
        in_specs=[SM, SM] + [VM] * 5,
        out_specs=(VM, VM, VM),
        scratch_shapes=[
            pltpu.VMEM((16, TILE, WIDE), jnp.float32),
            pltpu.VMEM((NY * NZ, TILE, WIDE), jnp.float32),
            pltpu.VMEM((2, 8, HD), jnp.float32),
        ],
        compiler_params=pltpu.CompilerParams(vmem_limit_bytes=VMEM_LIMIT),
    )(pairs, scale, rgbx, cotx, pose, rs, fin)


def output_kernel(
    rgbp, pp, sc,
    rgb_grad, pose_grad, scale_out,
    rbuf, sbuf, fbuf, s_z, s_y, s_t,
    local_sem, r_send, r_recv, z_send, z_recv, f_send, f_recv,
    sz_send, sz_recv, sy_send, sy_recv, st_send, st_recv,
):
    y, z = place()
    t = lax.axis_index("tm")
    greet(
        [((y + k) % NY, z) for k in range(1, NY)] + [(y, (z + k) % NZ) for k in range(1, NZ)],
        [(t + k) % NT for k in range(1, NT)],
    )

    def rgb_copy(k):
        to = (y + k) % NY
        src = rgbp.at[pl.ds(to * 4, 4)]
        dst = rgb_grad.at[:, :, columns(y)]
        if k == 0:
            return pltpu.make_async_copy(src, dst, local_sem.at[0])
        return remote(src, dst, r_send.at[k - 1], r_recv.at[k - 1], to, z)

    def hop(side, step, c, direct):
        to = (z + 1) % NZ if side == 0 else (z + NZ - 1) % NZ
        src = pp.at[goal(side, step) * NY + (y + c) % NY] if direct else sbuf.at[side, step, c]
        return remote(
            src, rbuf.at[side, step, c], z_send.at[side, step, c], z_recv.at[side, step, c], y, to
        )

    def goal(side, step):
        return (z + 4 - step) % NZ if side == 0 else (z + 4 + step) % NZ

    def used(side, step, c):
        return step > 0 or (c < 2) == (side == 0)

    def z_scale(k):
        return remote(sc, s_z.at[z], sz_send.at[k - 1], sz_recv.at[k - 1], y, (z + k) % NZ)

    def y_scale(k):
        ref = s_y.at[y]
        return remote(ref, ref, sy_send.at[k - 1], sy_recv.at[k - 1], (y + k) % NY, z)

    def t_scale(k):
        ref = s_t.at[t]
        return remote_tm(ref, ref, st_send.at[k - 1], st_recv.at[k - 1], (t + k) % NT)

    order = (1, 2, 3, 0)
    sent = []
    for c in order:
        for side in range(2):
            if used(side, 0, c):
                copy = hop(side, 0, c, True)
                copy.start()
                sent.append(copy)
    for k in range(1, NZ):
        z_scale(k).start()
    for k in range(NY):
        rgb_copy(k).start()
    s_z[z] = sc[...]
    for step in range(1, 4):
        for c in order:
            for side in range(2):
                direct = not used(side, step - 1, c)
                if not direct:
                    hop(side, step - 1, c, True).wait_recv()
                    mine = pp[goal(side, step) * NY + (y + c) % NY].astype(jnp.float32)
                    sbuf[side, step, c] = (
                        rbuf[side, step - 1, c].astype(jnp.float32) + mine
                    ).astype(jnp.bfloat16)
                copy = hop(side, step, c, direct)
                copy.start()
                sent.append(copy)
        if step == 1:
            for k in range(1, NZ):
                z_scale(k).wait_recv()
            total = s_z[0]
            for k in range(1, NZ):
                total = total + s_z[k]
            s_y[y] = total
            for k in range(1, NY):
                y_scale(k).start()
        if step == 2:
            for k in range(1, NY):
                y_scale(k).wait_recv()
            row = lax.broadcasted_iota(jnp.int32, (8, HD), 0)
            total = jnp.zeros((8, HD), jnp.float32)
            for k in range(NY):
                for h in range(2):
                    total = jnp.where(row == 2 * k + h, s_y[k, h:h + 1, :], total)
            s_t[t] = total
            for k in range(1, NT):
                t_scale(k).start()

    def final(k):
        to = (y + k) % NY
        src = fbuf.at[k]
        dst = pose_grad.at[:, columns(y)]
        if k == 0:
            return pltpu.make_async_copy(src, dst, local_sem.at[1])
        return remote(src, dst, f_send.at[k - 1], f_recv.at[k - 1], to, z)

    for c in order:
        for side in range(2):
            hop(side, 3, c, False).wait_recv()
        mine = pp[z * NY + (y + c) % NY].astype(jnp.float32)
        fbuf[c] = (
            rbuf[0, 3, c].astype(jnp.float32) + rbuf[1, 3, c].astype(jnp.float32) + mine
        ).astype(jnp.bfloat16)
        final(c).start()
    for k in range(1, NT):
        t_scale(k).wait_recv()
    total = s_t[0]
    for k in range(1, NT):
        total = total + s_t[k]
    scale_out[...] = total
    for k in range(1, NY):
        rgb_copy(k).wait()
        final(k).wait()
        y_scale(k).wait_send()
    rgb_copy(0).wait()
    final(0).wait()
    for k in range(1, NZ):
        z_scale(k).wait_send()
    for k in range(1, NT):
        t_scale(k).wait_send()
    for copy in sent:
        copy.wait_send()


def output(rgbp, pp, sc):
    dma = pltpu.SemaphoreType.DMA
    return pl.pallas_call(
        output_kernel,
        out_shape=(
            jax.ShapeDtypeStruct((4, TILE, 1024), jnp.bfloat16),
            jax.ShapeDtypeStruct((TILE, 1024), jnp.bfloat16),
            jax.ShapeDtypeStruct((8, HD), jnp.float32),
        ),
        in_specs=[ANY, VM, VM],
        out_specs=(ANY, ANY, VM),
        scratch_shapes=[
            pltpu.VMEM((2, 4, NY, TILE, WIDE), jnp.bfloat16),
            pltpu.VMEM((2, 4, NY, TILE, WIDE), jnp.bfloat16),
            pltpu.VMEM((NY, TILE, WIDE), jnp.bfloat16),
            pltpu.VMEM((NZ, 8, HD), jnp.float32),
            pltpu.VMEM((NY, 8, HD), jnp.float32),
            pltpu.VMEM((NT, 8, HD), jnp.float32),
            dma((2,)),
            dma((NY - 1,)), dma((NY - 1,)),
            dma((2, 4, NY)), dma((2, 4, NY)),
            dma((NY - 1,)), dma((NY - 1,)),
            dma((NZ - 1,)), dma((NZ - 1,)),
            dma((NY - 1,)), dma((NY - 1,)),
            dma((NT - 1,)), dma((NT - 1,)),
        ],
        compiler_params=pltpu.CompilerParams(
            collective_id=2, has_side_effects=True, vmem_limit_bytes=VMEM_LIMIT
        ),
    )(rgbp, pp, sc)


def local(rgb_feat, rgb_grad_out, pose_feat, pose_grad_out, logit_scale, pairs):
    y, _ = place()
    scale = lax.dynamic_slice(logit_scale, (2 * y,), (2,))
    rgbx, cotx, pose, codes = gather(
        rgb_feat.reshape(4, TILE, 1024),
        rgb_grad_out.reshape(4, TILE, 1024),
        pose_feat[0],
        pose_grad_out[0],
        pairs,
    )
    st, rs = stats(codes, scale, rgbx, cotx, pose)
    fin = exchange(st)
    rgbp, pp, sc = backward(codes, scale, rgbx, cotx, pose, rs, fin)
    rgb_grad, pose_grad, scale_grad = output(rgbp, pp, sc)
    return rgb_grad.reshape(1, 512, 1024), pose_grad[None], scale_grad[:, 0]


def solution(mesh):
    return jax.shard_map(
        local,
        mesh=mesh,
        in_specs=(
            P("tm", "seq", None),
            P("tm", "seq", None),
            P("tm", "seq", None),
            P("tm", "seq", None),
            P(),
            P("tm", "seq"),
        ),
        out_specs=(P("tm", "seq", None), P("tm", "seq", None), P()),
        check_vma=False,
    )
```

time: 797 us -> 132 us (0.17)
  waiting for transfers between devices: 491 us -> 0 us
  Pallas kernels: 0 us -> 125 us
  local copies, waits for them, and re-layouts: 97 us -> 6.47 us
  blocking collectives: 73.8 us -> 0 us
  other arithmetic: 70 us -> 0 us
  matrix products: 47.1 us -> 0 us
  between operations: 14.1 us -> 0.68 us
    all_gather x4 -> x0, waiting for transfers between devices: 348 us -> none  [the longest x3 206 us: merged(): gathered = jax.tree.map(lambda a: lax.all_gather(a, axis), part)]
    reduce_scatter x1 -> x0, waiting for transfers between devices: 142 us -> none  [local(): lax.psum_scatter(pose_terms.astype(jnp.bfloat16), 'seq', scatter_dimensio...]
    pallas_call x0 -> x5, Pallas kernels: none -> 125 us  [the longest x1 55.1 us: gather(): pl.pallas_call(gather_kernel, out_shape=(jax.ShapeDtypeStruct((16, TILE,...]
    psum x1 -> x0, blocking collectives: 73.8 us -> none  [local(): scale_grad = lax.psum(scale_term, ('tm', 'seq'))]
    add x62 -> x0, other arithmetic: 63.8 us -> none  [the longest x31 32.1 us: merge_stats(): former[2] * former_scale + latter[2] * latter_scale]
    dot_general x15 -> x0, matrix products: 47.1 us -> none  [the longest x9 29.8 us: product(): jnp.einsum(pattern, former, latter, preferred_element_type=jnp.float32)]
    dynamic_slice x34 -> x1, local copies, waits for them, and re-layouts: 33.7 us -> 1.24 us  [local(): scale = lax.dynamic_slice(logit_scale, (2 * y,), (2,))]
    gather x14 -> x0, local copies, waits for them, and re-layouts: 23 us -> none  [the longest x2 7.63 us: local(): pose_blocks = pose_all[pose_index]]
  transfers between devices with their start and end apart: 5 -> 0, of which waited for: 5 -> 0; matrix products, arithmetic and copies ran while one was open for 6% -> 0% of each run, Pallas kernels for 0% -> 0%
where the time goes in v1:
time: 132 us
  Pallas kernels  125 us (95%)
  local copies, waits for them, and re-layouts  6.47 us (5%)
    pallas_call x1, Pallas kernels, gather(): pl.pallas_call(gather_kernel, out_shape=(jax.ShapeDtypeStruct((16, TILE,...  55.1 us
    pallas_call x1, Pallas kernels, output(): pl.pallas_call(output_kernel, out_shape=(jax.ShapeDtypeStruct((4, TILE, 1...  33 us
    pallas_call x1, Pallas kernels, exchange(): pl.pallas_call(exchange_kernel, out_shape=jax.ShapeDtypeStruct((NY * NZ,...  14.7 us
    pallas_call x1, Pallas kernels, backward(): pl.pallas_call(backward_kernel, out_shape=(jax.ShapeDtypeStruct((16, TILE...  14.5 us
    pallas_call x1, Pallas kernels, stats(): pl.pallas_call(stats_kernel, out_shape=(jax.ShapeDtypeStruct((NY * NZ, 8,...  7.53 us
    unnamed x2, local copies, waits for them, and re-layouts  3.93 us

profile of v1, /device:TPU:2, one launch (start us, length us, event | category | flops | bytes accessed | tf_op | source)
XLA Modules:
  0.0 132.0 jit_solution(6075295589316753096)
XLA Ops:
  0.6 1.2 dynamic_slice.3.scale
  1.9 55.1 %shard_map.85 = (bf16[16,128,256]{2,1,0:T(8,128)(2,1)}, bf16[16,128,256]{2,1,0:T(8,128)(2,1)}, bf16[32,2,128,256]{3,2,1,0:T(8,128)(2,1)}, s32[4,1,5]{2,1,0:T(1,128)}) custom-call(bf16[4,128,1024]{2,1,0:T(8,128)(2,1)} %bitcast.6, bf16[4,128,1024]{2,1,0:T(8,128)(2,1)} %bitcast.7, bf16[128,1024]{1,0:T(8,128)(2,1)} %bitcast.10, bf16[128,1024]{1,0:T(8,128)(2,1)} %bitcast.11, ...), custom_call_target="tpu_custom_call" | custom-call | tf_op jit(solution)/shard_map/pallas_call | solution.py:156
  57.0 7.5 %shard_map.86 = (f32[32,8,128]{2,1,0:T(8,128)}, f32[16,8,128]{2,1,0:T(8,128)}) custom-call(s32[4,1,5]{2,1,0:T(1,128)} %get-tuple-element.15.pairs, f32[2]{0:T(128)} %dynamic_slice.3.scale, bf16[16,128,256]{2,1,0:T(8,128)(2,1)} %get-tuple-element.16.rgbx, bf16[16,128,256]{2,1,0:T(8,128)(2,1)} %get-tuple-element.17.cotx, ...), custom_call_target="tpu_custom_call" | custom-call | tf_op jit(solution)/shard_map/pallas_call | solution.py:244
  64.6 14.7 %shard_map.87.fin = f32[32,8,128]{2,1,0:T(8,128)} custom-call(f32[32,8,128]{2,1,0:T(8,128)} %get-tuple-element.20.st), custom_call_target="tpu_custom_call" | custom-call | tf_op jit(solution)/shard_map/pallas_call | solution.py:301
  79.2 14.5 %shard_map.88 = (bf16[16,128,256]{2,1,0:T(8,128)(2,1)}, bf16[32,128,256]{2,1,0:T(8,128)(2,1)}, f32[8,128]{1,0:T(8,128)}) custom-call(s32[4,1,5]{2,1,0:T(1,128)} %get-tuple-element.15.pairs, f32[2]{0:T(128)} %dynamic_slice.3.scale, bf16[16,128,256]{2,1,0:T(8,128)(2,1)} %get-tuple-element.16.rgbx, bf16[16,128,256]{2,1,0:T(8,128)(2,1)} %get-tuple-element.17.cotx, ...), custom_call_target="tpu_custom_call" | custom-call | tf_op jit(solution)/shard_map/pallas_call | solution.py:376
  93.8 33.0 %shard_map.89 = (bf16[4,128,1024]{2,1,0:T(8,128)(2,1)}, bf16[128,1024]{1,0:T(8,128)(2,1)}, f32[8,128]{1,0:T(8,128)}) custom-call(bf16[16,128,256]{2,1,0:T(8,128)(2,1)} %get-tuple-element.21.rgbp, bf16[32,128,256]{2,1,0:T(8,128)(2,1)} %get-tuple-element.22.pp, f32[8,128]{1,0:T(8,128)} %get-tuple-element.23.sc), custom_call_target="tpu_custom_call" | custom-call | tf_op jit(solution)/shard_map/pallas_call | solution.py:525
  126.8 1.3 slice_reduce_fusion
  128.1 2.3 %copy.11 = bf16[1,512,1024]{2,1,0:T(8,128)(2,1)} copy(bf16[1,512,1024]{2,1,0:T(8,128)(2,1)} %bitcast.8) | data formatting | bytes 2097152
  130.3 1.7 %copy.12 = bf16[1,128,1024]{2,1,0:T(8,128)(2,1)} copy(bf16[1,128,1024]{2,1,0:T(8,128)(2,1)} %bitcast.9) | data formatting | bytes 524288

commit v2 on v0

v2 whole, which is shorter than its diff:
```python
import math

import jax
import jax.numpy as jnp
from jax import lax
from jax.experimental import pallas as pl
from jax.experimental.pallas import tpu as pltpu
from jax.sharding import PartitionSpec as P

NEG = -1e30
NY = 4
NZ = 8
NT = 8
TILE = 128
HD = 128
SLOTS = 5
COUNT = NY * SLOTS
VMEM_LIMIT = 56 * 1024 * 1024
MESH = pl.DeviceIdType.MESH
ANY = pl.BlockSpec(memory_space=pl.ANY)
VM = pl.BlockSpec(memory_space=pltpu.VMEM)
SM = pl.BlockSpec(memory_space=pltpu.SMEM)
POSE, RGB, POSE_KEY, RGB_KEY, POSE_PREV, RGB_PREV, RGB_LAST, POSE_END, RGB_END = range(9)
ORDER = (1, 2, 3, 0)


def place():
    me = lax.axis_index("seq")
    return me // NZ, me % NZ


def remote(src, dst, send_sem, recv_sem, y, z):
    return pltpu.make_async_remote_copy(
        src_ref=src,
        dst_ref=dst,
        send_sem=send_sem,
        recv_sem=recv_sem,
        device_id={"seq": y * NZ + z},
        device_id_type=MESH,
    )


def remote_tm(src, dst, send_sem, recv_sem, t):
    return pltpu.make_async_remote_copy(
        src_ref=src,
        dst_ref=dst,
        send_sem=send_sem,
        recv_sem=recv_sem,
        device_id={"tm": t},
        device_id_type=MESH,
    )


def greet(seqs, tms=()):
    barrier = pltpu.get_barrier_semaphore()
    for y, z in seqs:
        pl.semaphore_signal(
            barrier, inc=1, device_id={"seq": y * NZ + z}, device_id_type=MESH
        )
    for t in tms:
        pl.semaphore_signal(barrier, inc=1, device_id={"tm": t}, device_id_type=MESH)
    pl.semaphore_wait(barrier, len(seqs) + len(tms))


def columns(y, h):
    return pl.ds(pl.multiple_of((2 * y + h) * HD, HD), HD)


def dot_t(a, b):
    return lax.dot_general(a, b, (((1,), (1,)), ((), ())), preferred_element_type=jnp.float32)


def fill_table(codes, tab):
    def slots(n, carry):
        pos = (n // 10) * 2 + n % 2
        code = codes[pos, 0, (n % 10) // 2]
        kept = jnp.maximum(code, 0)
        tile = kept % (NY * NZ)
        pi = (tile % NZ) * NY + tile // NZ
        ri = pos * 4 + kept // (NY * NZ)
        tab[POSE, n] = pi
        tab[RGB, n] = ri
        tab[POSE_KEY, n] = jnp.where(code >= 0, pi, -1 - n)
        tab[RGB_KEY, n] = jnp.where(code >= 0, ri, -1 - n)
        return carry

    lax.fori_loop(0, COUNT, slots, 0)

    def chains(n, carry):
        pose_key, rgb_key = tab[POSE_KEY, n], tab[RGB_KEY, n]
        pose_prev, rgb_prev, rgb_last = COUNT, COUNT, COUNT
        for m in range(COUNT):
            same_rgb = tab[RGB_KEY, m] == rgb_key
            early = n > m
            pose_prev = jnp.where((tab[POSE_KEY, m] == pose_key) & early, m, pose_prev)
            rgb_prev = jnp.where(same_rgb & early, m, rgb_prev)
            rgb_last = jnp.where(same_rgb, m, rgb_last)
        tab[POSE_PREV, n] = pose_prev
        tab[RGB_PREV, n] = rgb_prev
        tab[RGB_LAST, n] = rgb_last
        return carry

    lax.fori_loop(0, COUNT, chains, 0)

    def ends(p, carry):
        pose_end, rgb_end = COUNT, COUNT
        for m in range(COUNT):
            pose_end = jnp.where(tab[POSE_KEY, m] == p, m, pose_end)
            rgb_end = jnp.where(tab[RGB_KEY, m] == p, m, rgb_end)
        tab[POSE_END, p] = pose_end
        tab[RGB_END, p] = rgb_end
        return carry

    lax.fori_loop(0, NY * NZ, ends, 0)


def merge(ref, n, before, high, total, inner):
    old = ref[before, 0:1, :]
    top = jnp.maximum(old, high)
    keep = jnp.exp(old - top)
    add = jnp.exp(high - top)
    ref[n, 0:1, :] = top
    ref[n, 1:2, :] = ref[before, 1:2, :] * keep + total * add
    ref[n, 2:3, :] = ref[before, 2:3, :] * keep + inner * add


def slot_stats(n, tab, factor, rgbx, cotx, pose, st, rs):
    pi, ri = tab[POSE, n], tab[RGB, n]
    q = rgbx[ri]
    g = cotx[ri]
    both = pose[pi].reshape(2 * TILE, HD)
    pf = pose[pi, 0]
    dots = dot_t(q, both)
    score = dots[:, :TILE] * factor
    high = jnp.max(score, axis=0, keepdims=True)
    w = jnp.exp(score - high)
    pose_new = (
        high,
        jnp.sum(w, axis=0, keepdims=True),
        jnp.sum(w * dots[:, TILE:], axis=0, keepdims=True),
    )
    score = dot_t(pf, q) * factor
    grad = dot_t(pf, g)
    high = jnp.max(score, axis=0, keepdims=True)
    w = jnp.exp(score - high)
    rgb_new = (
        high,
        jnp.sum(w, axis=0, keepdims=True),
        jnp.sum(w * grad, axis=0, keepdims=True),
    )
    return pose_new, rgb_new


def slot_backward(n, tab, factor, rgbx, cotx, pose, rs, fin):
    pi, ri = tab[POSE, n], tab[RGB, n]
    last = tab[RGB_LAST, n]
    inverse = 1.0 / jnp.maximum(rs[last, 1:2, :], 1.0)
    rows = jnp.concatenate(
        [rs[last, 0:1, :], inverse, rs[last, 2:3, :] * inverse, jnp.zeros((5, HD), jnp.float32)],
        axis=0,
    )
    rows = jnp.transpose(rows)
    zz, yy = pi // NY, pi % NY
    q = rgbx[ri]
    g = cotx[ri]
    both = pose[pi].reshape(2 * TILE, HD)
    pf = pose[pi, 0]
    pc = pose[pi, 1]
    dots = dot_t(q, both)
    raw = dots[:, :TILE]
    score = raw * factor
    grad = dot_t(g, pf)
    pr = jnp.exp(score - rows[:, 0:1]) * rows[:, 1:2]
    pp = jnp.exp(score - fin[zz, pl.ds(yy, 1), :]) * fin[zz, pl.ds(4 + yy, 1), :]
    ds = pr * (grad - rows[:, 2:3]) + pp * (dots[:, TILE:] - fin[zz, pl.ds(8 + yy, 1), :])
    scale_part = jnp.sum((ds * raw).reshape(TILE // 8, 8, HD), axis=0)
    scale_part = jnp.where(tab[POSE_KEY, n] >= 0, scale_part, 0.0)
    ds_low = ds.astype(jnp.bfloat16)
    pr_low = pr.astype(jnp.bfloat16)
    pp_low = pp.astype(jnp.bfloat16)
    rgb_part = jnp.dot(pp_low, pc, preferred_element_type=jnp.float32) + factor * jnp.dot(
        ds_low, pf, preferred_element_type=jnp.float32
    )
    turned = (((0,), (0,)), ((), ()))
    pose_part = lax.dot_general(
        pr_low, g, turned, preferred_element_type=jnp.float32
    ) + factor * lax.dot_general(ds_low, q, turned, preferred_element_type=jnp.float32)
    return rgb_part, pose_part, scale_part


def fused_kernel(
    rgb_ref, cot_ref, pf_ref, pc_ref, pairs_ref, scale,
    rgb_grad, pose_grad, scale_out, pairs_x,
    rgbx, cotx, pose, st, rs, ex, got, fin, racc, pacc, sacc,
    rgbs, rbuf, sbuf, fbuf, sc, s_z, s_y, s_t, codes, tab,
    own_sem, codes_sem, y_send, y_recv, z_send, z_recv,
    e1_send, e1_recv, e2_send, e2_recv,
    o_own, o_send, o_recv, r_send, r_recv, f_own, f_send, f_recv,
    sz_send, sz_recv, sy_send, sy_recv, st_send, st_recv,
):
    y, z = place()
    t = lax.axis_index("tm")
    sent = []

    def start(copy):
        copy.start()
        sent.append(copy)

    def y_parts(k):
        to = (y + k) % NY
        pos = 3 - k
        parts = [(pairs_ref, pairs_x.at[pos])]
        for h in range(2):
            cols = columns(to, h)
            parts += [
                (pf_ref.at[:, cols], pose[h].at[z * NY + y, 0]),
                (pc_ref.at[:, cols], pose[h].at[z * NY + y, 1]),
                (rgb_ref.at[:, :, cols], rgbx[h].at[pl.ds(pos * 4, 4)]),
                (cot_ref.at[:, :, cols], cotx[h].at[pl.ds(pos * 4, 4)]),
            ]
        return parts

    def own(i):
        src, dst = y_parts(0)[i]
        return pltpu.make_async_copy(src, dst, own_sem.at[i])

    def across(k, i):
        src, dst = y_parts(k)[i]
        return remote(src, dst, y_send.at[k - 1, i], y_recv.at[k - 1, i], (y + k) % NY, z)

    def hop(h, side, step, c):
        block = (z + NZ - step) % NZ if side == 0 else (z + step) % NZ
        to = (z + 1) % NZ if side == 0 else (z + NZ - 1) % NZ
        ref = pose[h].at[block * NY + (y + NY - c) % NY]
        return remote(
            ref, ref, z_send.at[h, side, step, c], z_recv.at[h, side, step, c], y, to
        )

    def last_used(side, c):
        return (c < 2) == (side == 0)

    def ring(h, step):
        for c in range(NY):
            if step == 0:
                for i in (1 + 4 * h, 2 + 4 * h):
                    if c == 0:
                        own(i).wait()
                    else:
                        across(c, i).wait_recv()
            for side in range(2):
                if step > 0:
                    hop(h, side, step - 1, c).wait_recv()
                if step < 3 or last_used(side, c):
                    start(hop(h, side, step, c))

    def ring_end(h):
        for c in range(NY):
            for side in range(2):
                if last_used(side, c):
                    hop(h, side, 3, c).wait_recv()

    def rgb_arrived(h):
        for i in (3 + 4 * h, 4 + 4 * h):
            for k in (1, 2, 3):
                across(k, i).wait_recv()
            own(i).wait()

    factor = [scale[2 * y + h] / math.sqrt(HD) for h in range(2)]

    def stats(h, low, high):
        def body(m, carry):
            news = [
                slot_stats(2 * m + u, tab, factor[h], rgbx[h], cotx[h], pose[h], st[h], rs[h])
                for u in range(2)
            ]
            for u in range(2):
                n = 2 * m + u
                merge(st[h], n, tab[POSE_PREV, n], *news[u][0])
                merge(rs[h], n, tab[RGB_PREV, n], *news[u][1])
            return carry

        lax.fori_loop(low, high, body, 0)

    def backward(h, low, high):
        def body(m, carry):
            news = [
                slot_backward(2 * m + u, tab, factor[h], rgbx[h], cotx[h], pose[h], rs[h], fin[h])
                for u in range(2)
            ]
            for u in range(2):
                n = 2 * m + u
                racc[h][n] = racc[h][tab[RGB_PREV, n]] + news[u][0]
                pacc[h][n] = pacc[h][tab[POSE_PREV, n]] + news[u][1]
            sacc[h] += news[0][2] + news[1][2]
            return carry

        lax.fori_loop(low, high, body, 0)

    def ex_copy(h, k):
        to = (z + k) % NZ
        return remote(
            ex[h].at[to], got[h].at[z], e1_send.at[h, k - 1], e1_recv.at[h, k - 1], y, to
        )

    def fin_copy(h, k):
        ref = fin[h].at[z]
        return remote(ref, ref, e2_send.at[h, k - 1], e2_recv.at[h, k - 1], y, (z + k) % NZ)

    def ex_first(h):
        def pack(zz, carry):
            for yy in range(NY):
                last = tab[POSE_END, zz * NY + yy]
                for i in range(3):
                    ex[h][zz, 4 * i + yy:4 * i + yy + 1, :] = st[h][last, i:i + 1, :]
            return carry

        lax.fori_loop(0, NZ, pack, 0)
        for k in range(1, NZ):
            start(ex_copy(h, k))
        got[h][z] = ex[h][z]

    def ex_second(h):
        for k in range(1, NZ):
            ex_copy(h, k).wait_recv()
        top = got[h][0, 0:4, :]
        for k in range(1, NZ):
            top = jnp.maximum(top, got[h][k, 0:4, :])
        total = jnp.zeros_like(top)
        inner = jnp.zeros_like(top)
        for k in range(NZ):
            keep = jnp.exp(got[h][k, 0:4, :] - top)
            total += got[h][k, 4:8, :] * keep
            inner += got[h][k, 8:12, :] * keep
        inverse = 1.0 / jnp.maximum(total, 1.0)
        fin[h][z, 0:4, :] = top
        fin[h][z, 4:8, :] = inverse
        fin[h][z, 8:12, :] = inner * inverse
        for k in range(1, NZ):
            start(fin_copy(h, k))

    def ex_end(h):
        for k in range(1, NZ):
            fin_copy(h, k).wait_recv()

    def rgb_copy(h, pos):
        src = rgbs[h].at[pos]
        dst = rgb_grad.at[:, :, columns(y, h)]
        if pos == 3:
            return pltpu.make_async_copy(src, dst, o_own.at[h])
        return remote(src, dst, o_send.at[h, pos], o_recv.at[h, pos], (y + 1 + pos) % NY, z)

    def rgb_send(h, pos):
        for i in range(4):
            rgbs[h][pos, i] = racc[h][tab[RGB_END, pos * 4 + i]].astype(jnp.bfloat16)
        rgb_copy(h, pos).start()

    def goal(side, step):
        return (z + 4 - step) % NZ if side == 0 else (z + 4 + step) % NZ

    def back(h, side, step, c):
        to = (z + 1) % NZ if side == 0 else (z + NZ - 1) % NZ
        return remote(
            sbuf[h].at[side, step, c], rbuf[h].at[side, step, c],
            r_send.at[h, side, step, c], r_recv.at[h, side, step, c], y, to,
        )

    def mine(h, block, c):
        return pacc[h][tab[POSE_END, block * NY + (y + c) % NY]]

    def back_step(h, step):
        for c in ORDER:
            for side in range(2):
                if step == 0 and not last_used(side, c):
                    continue
                value = mine(h, goal(side, step), c)
                if step > 1 or (step == 1 and last_used(side, c)):
                    back(h, side, step - 1, c).wait_recv()
                    value = value + rbuf[h][side, step - 1, c].astype(jnp.float32)
                sbuf[h][side, step, c] = value.astype(jnp.bfloat16)
                start(back(h, side, step, c))

    def final(h, c):
        src = fbuf[h].at[c]
        dst = pose_grad.at[:, columns(y, h)]
        if c == 0:
            return pltpu.make_async_copy(src, dst, f_own.at[h])
        return remote(src, dst, f_send.at[h, c - 1], f_recv.at[h, c - 1], (y + c) % NY, z)

    def back_end(h):
        for c in ORDER:
            value = mine(h, z, c)
            for side in range(2):
                back(h, side, 3, c).wait_recv()
                value = value + rbuf[h][side, 3, c].astype(jnp.float32)
            fbuf[h][c] = value.astype(jnp.bfloat16)
            final(h, c).start()

    def z_scale(k):
        return remote(sc, s_z.at[z], sz_send.at[k - 1], sz_recv.at[k - 1], y, (z + k) % NZ)

    def y_scale(k):
        ref = s_y.at[y]
        return remote(ref, ref, sy_send.at[k - 1], sy_recv.at[k - 1], (y + k) % NY, z)

    def t_scale(k):
        ref = s_t.at[t]
        return remote_tm(ref, ref, st_send.at[k - 1], st_recv.at[k - 1], (t + k) % NT)

    def total_of(ref, count):
        total = ref[0]
        for k in range(1, count):
            total = total + ref[k]
        return total

    def scale_first():
        lane = lax.broadcasted_iota(jnp.int32, (8, HD), 1)
        tile = jnp.zeros((8, HD), jnp.float32)
        for h in range(2):
            part = jnp.sum(sacc[h], axis=0, keepdims=True)
            part = jnp.sum(part, axis=1, keepdims=True) / math.sqrt(HD)
            tile = jnp.where(lane == 2 * y + h, part, tile)
        sc[...] = tile
        for k in range(1, NZ):
            start(z_scale(k))
        s_z[z] = tile

    def scale_second():
        for k in range(1, NZ):
            z_scale(k).wait_recv()
        s_y[y] = total_of(s_z, NZ)
        for k in range(1, NY):
            start(y_scale(k))

    def scale_third():
        for k in range(1, NY):
            y_scale(k).wait_recv()
        s_t[t] = total_of(s_y, NY)
        for k in range(1, NT):
            start(t_scale(k))

    def scale_end():
        for k in range(1, NT):
            t_scale(k).wait_recv()
        scale_out[...] = total_of(s_t, NT)

    greet(
        [((y + k) % NY, z) for k in range(1, NY)] + [(y, (z + k) % NZ) for k in range(1, NZ)],
        [(t + k) % NT for k in range(1, NT)],
    )
    for i in (1, 2):
        own(i).start()
    for i in (1, 2, 0, 5, 6):
        for k in (1, 2, 3):
            start(across(k, i))
    for i in (0, 5, 6):
        own(i).start()
    for h in range(2):
        st[h][COUNT, 0:1, :] = jnp.full((1, HD), NEG, jnp.float32)
        rs[h][COUNT, 0:1, :] = jnp.full((1, HD), NEG, jnp.float32)
        st[h][COUNT, 1:3, :] = jnp.zeros((2, HD), jnp.float32)
        rs[h][COUNT, 1:3, :] = jnp.zeros((2, HD), jnp.float32)
        racc[h][COUNT] = jnp.zeros((TILE, HD), jnp.float32)
        pacc[h][COUNT] = jnp.zeros((TILE, HD), jnp.float32)
        sacc[h] = jnp.zeros((8, HD), jnp.float32)
    ring(0, 0)
    for i in (3, 4, 7, 8):
        for k in (1, 2, 3):
            start(across(k, i))
        own(i).start()
    for k in (1, 2, 3):
        across(k, 0).wait_recv()
    own(0).wait()
    to_codes = pltpu.make_async_copy(pairs_x, codes, codes_sem.at[0])
    to_codes.start()
    to_codes.wait()
    ring(0, 1)
    fill_table(codes, tab)
    ring(0, 2)
    ring(0, 3)
    ring(1, 0)
    ring_end(0)
    rgb_arrived(0)
    stats(0, 0, 5)
    ring(1, 1)
    stats(0, 5, 10)
    ex_first(0)
    ring(1, 2)
    ex_second(0)
    ring(1, 3)
    ring_end(1)
    rgb_arrived(1)
    stats(1, 0, 10)
    ex_first(1)
    ex_end(0)
    backward(0, 0, 5)
    rgb_send(0, 0)
    rgb_send(0, 1)
    ex_second(1)
    backward(0, 5, 10)
    rgb_send(0, 2)
    rgb_send(0, 3)
    back_step(0, 0)
    ex_end(1)
    backward(1, 0, 5)
    rgb_send(1, 0)
    rgb_send(1, 1)
    back_step(0, 1)
    backward(1, 5, 10)
    back_step(1, 0)
    rgb_send(1, 2)
    rgb_send(1, 3)
    back_step(0, 2)
    scale_first()
    back_step(1, 1)
    back_step(0, 3)
    scale_second()
    back_step(1, 2)
    back_end(0)
    scale_third()
    back_step(1, 3)
    back_end(1)
    scale_end()
    for h in range(2):
        for pos in range(4):
            rgb_copy(h, pos).wait()
        for c in range(NY):
            final(h, c).wait()
    for copy in sent:
        copy.wait_send()


def fused(rgb, cot, pf, pc, pairs, scale):
    dma = pltpu.SemaphoreType.DMA
    low, full = jnp.bfloat16, jnp.float32

    def twice(shape, kind):
        return [pltpu.VMEM(shape, kind)] * 2

    return pl.pallas_call(
        fused_kernel,
        out_shape=(
            jax.ShapeDtypeStruct((4, TILE, 1024), low),
            jax.ShapeDtypeStruct((TILE, 1024), low),
            jax.ShapeDtypeStruct((8, HD), full),
            jax.ShapeDtypeStruct((NY, 1, SLOTS), jnp.int32),
        ),
        in_specs=[ANY] * 5 + [SM],
        out_specs=(ANY, ANY, VM, ANY),
        scratch_shapes=[
            twice((16, TILE, HD), low),
            twice((16, TILE, HD), low),
            twice((NY * NZ, 2, TILE, HD), low),
            twice((COUNT + 1, 8, HD), full),
            twice((COUNT + 1, 8, HD), full),
            twice((NZ, 16, HD), full),
            twice((NZ, 16, HD), full),
            twice((NZ, 16, HD), full),
            twice((COUNT + 1, TILE, HD), full),
            twice((COUNT + 1, TILE, HD), full),
            pltpu.VMEM((2, 8, HD), full),
            twice((4, 4, TILE, HD), low),
            twice((2, 4, NY, TILE, HD), low),
            twice((2, 4, NY, TILE, HD), low),
            twice((NY, TILE, HD), low),
            pltpu.VMEM((8, HD), full),
            pltpu.VMEM((NZ, 8, HD), full),
            pltpu.VMEM((NY, 8, HD), full),
            pltpu.VMEM((NT, 8, HD), full),
            pltpu.SMEM((NY, 1, SLOTS), jnp.int32),
            pltpu.SMEM((9, NY * NZ), jnp.int32),
            dma((9,)), dma((1,)), dma((3, 9)), dma((3, 9)),
            dma((2, 2, 4, NY)), dma((2, 2, 4, NY)),
            dma((2, NZ - 1)), dma((2, NZ - 1)), dma((2, NZ - 1)), dma((2, NZ - 1)),
            dma((2,)), dma((2, 3)), dma((2, 3)),
            dma((2, 2, 4, NY)), dma((2, 2, 4, NY)),
            dma((2,)), dma((2, 3)), dma((2, 3)),
            dma((NZ - 1,)), dma((NZ - 1,)),
            dma((NY - 1,)), dma((NY - 1,)),
            dma((NT - 1,)), dma((NT - 1,)),
        ],
        compiler_params=pltpu.CompilerParams(
            collective_id=0, has_side_effects=True, vmem_limit_bytes=VMEM_LIMIT
        ),
    )(rgb, cot, pf, pc, pairs, scale)


def local(rgb_feat, rgb_grad_out, pose_feat, pose_grad_out, logit_scale, pairs):
    rgb_grad, pose_grad, scale_grad, _ = fused(
        rgb_feat.reshape(4, TILE, 1024),
        rgb_grad_out.reshape(4, TILE, 1024),
        pose_feat[0],
        pose_grad_out[0],
        pairs,
        logit_scale,
    )
    return rgb_grad.reshape(1, 512, 1024), pose_grad[None], scale_grad[0, :8]


def solution(mesh):
    return jax.shard_map(
        local,
        mesh=mesh,
        in_specs=(
            P("tm", "seq", None),
            P("tm", "seq", None),
            P("tm", "seq", None),
            P("tm", "seq", None),
            P(),
            P("tm", "seq"),
        ),
        out_specs=(P("tm", "seq", None), P("tm", "seq", None), P()),
        check_vma=False,
    )
```

time: 797 us -> 109 us (0.14)
  waiting for transfers between devices: 491 us -> 0 us
  Pallas kernels: 0 us -> 102 us
  local copies, waits for them, and re-layouts: 97 us -> 4.2 us
  blocking collectives: 73.8 us -> 0 us
  other arithmetic: 70 us -> 0 us
  matrix products: 47.1 us -> 0 us
  between operations: 14.1 us -> 0.64 us
    all_gather x4 -> x0, waiting for transfers between devices: 348 us -> none  [the longest x3 206 us: merged(): gathered = jax.tree.map(lambda a: lax.all_gather(a, axis), part)]
    reduce_scatter x1 -> x0, waiting for transfers between devices: 142 us -> none  [local(): lax.psum_scatter(pose_terms.astype(jnp.bfloat16), 'seq', scatter_dimensio...]
    pallas_call x0 -> x1, Pallas kernels: none -> 102 us  [fused(): pl.pallas_call(fused_kernel, out_shape=(jax.ShapeDtypeStruct((4, TILE, 10...]
    psum x1 -> x0, blocking collectives: 73.8 us -> none  [local(): scale_grad = lax.psum(scale_term, ('tm', 'seq'))]
    add x62 -> x0, other arithmetic: 63.8 us -> none  [the longest x31 32.1 us: merge_stats(): former[2] * former_scale + latter[2] * latter_scale]
    dot_general x15 -> x0, matrix products: 47.1 us -> none  [the longest x9 29.8 us: product(): jnp.einsum(pattern, former, latter, preferred_element_type=jnp.float32)]
    dynamic_slice x34 -> x0, local copies, waits for them, and re-layouts: 33.7 us -> none  [take(): lax.dynamic_index_in_dim(a, source, 0, False)]
    gather x14 -> x0, local copies, waits for them, and re-layouts: 23 us -> none  [the longest x2 7.63 us: local(): pose_blocks = pose_all[pose_index]]
  transfers between devices with their start and end apart: 5 -> 0, of which waited for: 5 -> 0; matrix products, arithmetic and copies ran while one was open for 6% -> 0% of each run, Pallas kernels for 0% -> 0%
where the time goes in v2:
time: 109 us; the launch traced here: 107 us
  Pallas kernels  102 us (94%)
  local copies, waits for them, and re-layouts  4.2 us (4%)
    pallas_call x1, Pallas kernels, fused(): pl.pallas_call(fused_kernel, out_shape=(jax.ShapeDtypeStruct((4, TILE, 10...  102 us
    unnamed x4, local copies, waits for them, and re-layouts  3.01 us

profile of v2, /device:TPU:2, one launch (start us, length us, event | category | flops | bytes accessed | tf_op | source)
XLA Modules:
  0.0 107.3 jit_solution(1896603115611988291)
XLA Ops:
  0.6 102.4 %shard_map.85 = (bf16[4,128,1024]{2,1,0:T(8,128)(2,1)}, bf16[128,1024]{1,0:T(8,128)(2,1)}, f32[8,128]{1,0:T(8,128)}, s32[4,1,5]{2,1,0:T(1,128)}) custom-call(bf16[4,128,1024]{2,1,0:T(8,128)(2,1)} %bitcast.8, bf16[4,128,1024]{2,1,0:T(8,128)(2,1)} %bitcast.9, bf16[128,1024]{1,0:T(8,128)(2,1)} %bitcast.11, bf16[128,1024]{1,0:T(8,128)(2,1)} %bitcast.12, ...), custom_call_target="tpu_custom_call" | custom-call | tf_op jit(solution)/shard_map/pallas_call | solution.py:539
  103.1 1.2 %slice_bitcast_fusion = f32[8]{0:T(128)} fusion(f32[8,128]{1,0:T(8,128)} %get-tuple-element.8), kind=kLoop, calls=%fused_computation | loop fusion | bytes 64 | tf_op jit(solution)/shard_map/squeeze | solution.py:596
  104.3 0.0 copy-start
  104.3 2.3 %copy.11 = bf16[1,512,1024]{2,1,0:T(8,128)(2,1)} copy(bf16[1,512,1024]{2,1,0:T(8,128)(2,1)} %bitcast.10) | data formatting | bytes 2097152
  106.6 0.0 copy-done
  106.6 0.7 copy.12
Async XLA Ops:
  104.3 2.3 %copy-start = (bf16[128,1024]{1,0:T(8,128)(2,1)S(1)}, bf16[128,1024]{1,0:T(8,128)(2,1)}, u32[]{:S(2)}) copy-start(bf16[128,1024]{1,0:T(8,128)(2,1)} %get-tuple-element.7) | copy-start | bytes 786436

commit v3 on v2

--- a/solution.py
+++ b/solution.py
@@ -22,6 +22,9 @@
 SM = pl.BlockSpec(memory_space=pltpu.SMEM)
 POSE, RGB, POSE_KEY, RGB_KEY, POSE_PREV, RGB_PREV, RGB_LAST, POSE_END, RGB_END = range(9)
 ORDER = (1, 2, 3, 0)
+CHUNKS = (0, 1, 3, 2)
+STATS_UNROLL = 10
+UNROLL = 5
 
 
 def place():
@@ -124,10 +127,10 @@
     ref[n, 2:3, :] = ref[before, 2:3, :] * keep + inner * add
 
 
-def slot_stats(n, tab, factor, rgbx, cotx, pose, st, rs):
+def slot_stats(n, tab, factor, qg, pose):
     pi, ri = tab[POSE, n], tab[RGB, n]
-    q = rgbx[ri]
-    g = cotx[ri]
+    q = qg[ri, 0]
+    g = qg[ri, 1]
     both = pose[pi].reshape(2 * TILE, HD)
     pf = pose[pi, 0]
     dots = dot_t(q, both)
@@ -139,19 +142,22 @@
         jnp.sum(w, axis=0, keepdims=True),
         jnp.sum(w * dots[:, TILE:], axis=0, keepdims=True),
     )
-    score = dot_t(pf, q) * factor
-    grad = dot_t(pf, g)
+    dots = dot_t(pf, qg[ri].reshape(2 * TILE, HD))
+    score = dots[:, :TILE] * factor
     high = jnp.max(score, axis=0, keepdims=True)
     w = jnp.exp(score - high)
     rgb_new = (
         high,
         jnp.sum(w, axis=0, keepdims=True),
-        jnp.sum(w * grad, axis=0, keepdims=True),
+        jnp.sum(w * dots[:, TILE:], axis=0, keepdims=True),
     )
     return pose_new, rgb_new
 
 
-def slot_backward(n, tab, factor, rgbx, cotx, pose, rs, fin):
+TURNED = (((0,), (0,)), ((), ()))
+
+
+def slot_before(n, tab, factor, qg, pose, rs):
     pi, ri = tab[POSE, n], tab[RGB, n]
     last = tab[RGB_LAST, n]
     inverse = 1.0 / jnp.maximum(rs[last, 1:2, :], 1.0)
@@ -160,40 +166,43 @@
         axis=0,
     )
     rows = jnp.transpose(rows)
+    q = qg[ri, 0]
+    g = qg[ri, 1]
+    both = pose[pi].reshape(2 * TILE, HD)
+    dots = dot_t(q, both)
+    score = dots[:, :TILE] * factor
+    grad = dot_t(g, pose[pi, 0])
+    pr = jnp.exp(score - rows[:, 0:1]) * rows[:, 1:2]
+    own = pr * (grad - rows[:, 2:3])
+    part = lax.dot_general(
+        pr.astype(jnp.bfloat16), g, TURNED, preferred_element_type=jnp.float32
+    )
+    return score, own, dots[:, TILE:], part
+
+
+def slot_after(n, tab, factor, qg, pose, fin, keep):
+    pi, ri = tab[POSE, n], tab[RGB, n]
     zz, yy = pi // NY, pi % NY
-    q = rgbx[ri]
-    g = cotx[ri]
-    both = pose[pi].reshape(2 * TILE, HD)
-    pf = pose[pi, 0]
-    pc = pose[pi, 1]
-    dots = dot_t(q, both)
-    raw = dots[:, :TILE]
-    score = raw * factor
-    grad = dot_t(g, pf)
-    pr = jnp.exp(score - rows[:, 0:1]) * rows[:, 1:2]
+    score = keep[0, n]
     pp = jnp.exp(score - fin[zz, pl.ds(yy, 1), :]) * fin[zz, pl.ds(4 + yy, 1), :]
-    ds = pr * (grad - rows[:, 2:3]) + pp * (dots[:, TILE:] - fin[zz, pl.ds(8 + yy, 1), :])
-    scale_part = jnp.sum((ds * raw).reshape(TILE // 8, 8, HD), axis=0)
+    ds = keep[1, n] + pp * (keep[2, n] - fin[zz, pl.ds(8 + yy, 1), :])
+    scale_part = jnp.sum((ds * score).reshape(TILE // 8, 8, HD), axis=0)
     scale_part = jnp.where(tab[POSE_KEY, n] >= 0, scale_part, 0.0)
-    ds_low = ds.astype(jnp.bfloat16)
-    pr_low = pr.astype(jnp.bfloat16)
-    pp_low = pp.astype(jnp.bfloat16)
-    rgb_part = jnp.dot(pp_low, pc, preferred_element_type=jnp.float32) + factor * jnp.dot(
-        ds_low, pf, preferred_element_type=jnp.float32
-    )
-    turned = (((0,), (0,)), ((), ()))
-    pose_part = lax.dot_general(
-        pr_low, g, turned, preferred_element_type=jnp.float32
-    ) + factor * lax.dot_general(ds_low, q, turned, preferred_element_type=jnp.float32)
+    ds_low = (ds * factor).astype(jnp.bfloat16)
+    pair = jnp.concatenate([ds_low, pp.astype(jnp.bfloat16)], axis=1)
+    rgb_part = jnp.dot(
+        pair, pose[pi].reshape(2 * TILE, HD), preferred_element_type=jnp.float32
+    )
+    pose_part = lax.dot_general(ds_low, qg[ri, 0], TURNED, preferred_element_type=jnp.float32)
     return rgb_part, pose_part, scale_part
 
 
 def fused_kernel(
     rgb_ref, cot_ref, pf_ref, pc_ref, pairs_ref, scale,
     rgb_grad, pose_grad, scale_out, pairs_x,
-    rgbx, cotx, pose, st, rs, ex, got, fin, racc, pacc, sacc,
+    qg, pose, st, rs, keep, ex, got, fin, racc, pacc, sacc,
     rgbs, rbuf, sbuf, fbuf, sc, s_z, s_y, s_t, codes, tab,
-    own_sem, codes_sem, y_send, y_recv, z_send, z_recv,
+    own_sem, codes_sem, y_send, y_recv, z_send, z_recv, b_send, b_recv,
     e1_send, e1_recv, e2_send, e2_recv,
     o_own, o_send, o_recv, r_send, r_recv, f_own, f_send, f_recv,
     sz_send, sz_recv, sy_send, sy_recv, st_send, st_recv,
@@ -215,8 +224,8 @@
             parts += [
                 (pf_ref.at[:, cols], pose[h].at[z * NY + y, 0]),
                 (pc_ref.at[:, cols], pose[h].at[z * NY + y, 1]),
-                (rgb_ref.at[:, :, cols], rgbx[h].at[pl.ds(pos * 4, 4)]),
-                (cot_ref.at[:, :, cols], cotx[h].at[pl.ds(pos * 4, 4)]),
+                (rgb_ref.at[:, :, cols], qg[h].at[pl.ds(pos * 4, 4), 0]),
+                (cot_ref.at[:, :, cols], qg[h].at[pl.ds(pos * 4, 4), 1]),
             ]
         return parts
 
@@ -239,19 +248,27 @@
     def last_used(side, c):
         return (c < 2) == (side == 0)
 
-    def ring(h, step):
-        for c in range(NY):
-            if step == 0:
-                for i in (1 + 4 * h, 2 + 4 * h):
-                    if c == 0:
-                        own(i).wait()
-                    else:
-                        across(c, i).wait_recv()
-            for side in range(2):
-                if step > 0:
-                    hop(h, side, step - 1, c).wait_recv()
-                if step < 3 or last_used(side, c):
-                    start(hop(h, side, step, c))
+    def begin(h, side, i):
+        src, dst = y_parts(0)[1 + 4 * h + i]
+        to = (z + 1) % NZ if side == 0 else (z + NZ - 1) % NZ
+        return remote(src, dst, b_send.at[h, side, i], b_recv.at[h, side, i], y, to)
+
+    def ring(h, step, c):
+        if step == 0:
+            across(c, 1 + 4 * h).wait_recv()
+            across(c, 2 + 4 * h).wait_recv()
+        for side in range(2):
+            if step == 1 and c == 0:
+                begin(h, side, 0).wait_recv()
+                begin(h, side, 1).wait_recv()
+            elif step > 0:
+                hop(h, side, step - 1, c).wait_recv()
+            if step < 3 or last_used(side, c):
+                start(hop(h, side, step, c))
+
+    def ring_all(h, step):
+        for c in CHUNKS:
+            ring(h, step, c)
 
     def ring_end(h):
         for c in range(NY):
@@ -260,6 +277,8 @@
                     hop(h, side, 3, c).wait_recv()
 
     def rgb_arrived(h):
+        own(1 + 4 * h).wait()
+        own(2 + 4 * h).wait()
         for i in (3 + 4 * h, 4 + 4 * h):
             for k in (1, 2, 3):
                 across(k, i).wait_recv()
@@ -267,31 +286,37 @@
 
     factor = [scale[2 * y + h] / math.sqrt(HD) for h in range(2)]
 
-    def stats(h, low, high):
+    def stats(h):
         def body(m, carry):
-            news = [
-                slot_stats(2 * m + u, tab, factor[h], rgbx[h], cotx[h], pose[h], st[h], rs[h])
-                for u in range(2)
-            ]
-            for u in range(2):
-                n = 2 * m + u
-                merge(st[h], n, tab[POSE_PREV, n], *news[u][0])
-                merge(rs[h], n, tab[RGB_PREV, n], *news[u][1])
+            slots = [STATS_UNROLL * m + u for u in range(STATS_UNROLL)]
+            news = [slot_stats(n, tab, factor[h], qg[h], pose[h]) for n in slots]
+            for n, (pose_new, rgb_new) in zip(slots, news):
+                merge(st[h], n, tab[POSE_PREV, n], *pose_new)
+                merge(rs[h], n, tab[RGB_PREV, n], *rgb_new)
             return carry
 
+        lax.fori_loop(0, COUNT // STATS_UNROLL, body, 0)
+
+    def before(h, low, high):
+        def body(m, carry):
+            slots = [UNROLL * m + u for u in range(UNROLL)]
+            news = [slot_before(n, tab, factor[h], qg[h], pose[h], rs[h]) for n in slots]
+            for n, new in zip(slots, news):
+                for i in range(3):
+                    keep[i, n] = new[i]
+                pacc[h][n] = new[3]
+            return carry
+
         lax.fori_loop(low, high, body, 0)
 
-    def backward(h, low, high):
+    def after(h, low, high):
         def body(m, carry):
-            news = [
-                slot_backward(2 * m + u, tab, factor[h], rgbx[h], cotx[h], pose[h], rs[h], fin[h])
-                for u in range(2)
-            ]
-            for u in range(2):
-                n = 2 * m + u
-                racc[h][n] = racc[h][tab[RGB_PREV, n]] + news[u][0]
-                pacc[h][n] = pacc[h][tab[POSE_PREV, n]] + news[u][1]
-            sacc[h] += news[0][2] + news[1][2]
+            slots = [UNROLL * m + u for u in range(UNROLL)]
+            news = [slot_after(n, tab, factor[h], qg[h], pose[h], fin[h], keep) for n in slots]
+            for n, new in zip(slots, news):
+                racc[h][n] = racc[h][tab[RGB_PREV, n]] + new[0]
+                pacc[h][n] = pacc[h][tab[POSE_PREV, n]] + (pacc[h][n] + new[1])
+            sacc[h] += sum(new[2] for new in news)
             return carry
 
         lax.fori_loop(low, high, body, 0)
@@ -417,7 +442,7 @@
         tile = jnp.zeros((8, HD), jnp.float32)
         for h in range(2):
             part = jnp.sum(sacc[h], axis=0, keepdims=True)
-            part = jnp.sum(part, axis=1, keepdims=True) / math.sqrt(HD)
+            part = jnp.sum(part, axis=1, keepdims=True) / scale[2 * y + h]
             tile = jnp.where(lane == 2 * y + h, part, tile)
         sc[...] = tile
         for k in range(1, NZ):
@@ -447,12 +472,16 @@
         [((y + k) % NY, z) for k in range(1, NY)] + [(y, (z + k) % NZ) for k in range(1, NZ)],
         [(t + k) % NT for k in range(1, NT)],
     )
-    for i in (1, 2):
-        own(i).start()
-    for i in (1, 2, 0, 5, 6):
-        for k in (1, 2, 3):
-            start(across(k, i))
-    for i in (0, 5, 6):
+    for h in range(2):
+        for i in range(2):
+            for side in range(2):
+                start(begin(h, side, i))
+        for i in (1 + 4 * h, 2 + 4 * h):
+            for k in (1, 2, 3):
+                start(across(k, i))
+    for k in (1, 2, 3):
+        start(across(k, 0))
+    for i in (0, 1, 2, 5, 6):
         own(i).start()
     for h in range(2):
         st[h][COUNT, 0:1, :] = jnp.full((1, HD), NEG, jnp.float32)
@@ -462,7 +491,8 @@
         racc[h][COUNT] = jnp.zeros((TILE, HD), jnp.float32)
         pacc[h][COUNT] = jnp.zeros((TILE, HD), jnp.float32)
         sacc[h] = jnp.zeros((8, HD), jnp.float32)
-    ring(0, 0)
+    for c in CHUNKS[1:]:
+        ring(0, 0, c)
     for i in (3, 4, 7, 8):
         for k in (1, 2, 3):
             start(across(k, i))
@@ -473,49 +503,54 @@
     to_codes = pltpu.make_async_copy(pairs_x, codes, codes_sem.at[0])
     to_codes.start()
     to_codes.wait()
-    ring(0, 1)
+    ring_all(0, 1)
     fill_table(codes, tab)
-    ring(0, 2)
-    ring(0, 3)
-    ring(1, 0)
+    ring_all(0, 2)
+    ring_all(0, 3)
+    for c in CHUNKS[1:]:
+        ring(1, 0, c)
     ring_end(0)
+    ring_all(1, 1)
     rgb_arrived(0)
-    stats(0, 0, 5)
-    ring(1, 1)
-    stats(0, 5, 10)
+    stats(0)
     ex_first(0)
-    ring(1, 2)
+    ring(1, 2, CHUNKS[0])
+    ring(1, 2, CHUNKS[1])
+    before(0, 0, 1)
+    ring(1, 2, CHUNKS[2])
+    before(0, 1, 2)
+    ring(1, 2, CHUNKS[3])
+    before(0, 2, 3)
     ex_second(0)
-    ring(1, 3)
+    ring(1, 3, CHUNKS[0])
+    before(0, 3, 4)
+    for c in CHUNKS[1:]:
+        ring(1, 3, c)
+    ex_end(0)
+    after(0, 0, 4)
+    back_step(0, 0)
+    for pos in range(4):
+        rgb_send(0, pos)
     ring_end(1)
     rgb_arrived(1)
-    stats(1, 0, 10)
+    stats(1)
     ex_first(1)
-    ex_end(0)
-    backward(0, 0, 5)
-    rgb_send(0, 0)
-    rgb_send(0, 1)
+    back_step(0, 1)
+    before(1, 0, 2)
+    back_step(0, 2)
     ex_second(1)
-    backward(0, 5, 10)
-    rgb_send(0, 2)
-    rgb_send(0, 3)
-    back_step(0, 0)
+    before(1, 2, 4)
+    back_step(0, 3)
     ex_end(1)
-    backward(1, 0, 5)
-    rgb_send(1, 0)
-    rgb_send(1, 1)
-    back_step(0, 1)
-    backward(1, 5, 10)
+    after(1, 0, 4)
     back_step(1, 0)
-    rgb_send(1, 2)
-    rgb_send(1, 3)
-    back_step(0, 2)
+    for pos in range(4):
+        rgb_send(1, pos)
     scale_first()
+    back_end(0)
     back_step(1, 1)
-    back_step(0, 3)
     scale_second()
     back_step(1, 2)
-    back_end(0)
     scale_third()
     back_step(1, 3)
     back_end(1)
@@ -547,11 +582,11 @@
         in_specs=[ANY] * 5 + [SM],
         out_specs=(ANY, ANY, VM, ANY),
         scratch_shapes=[
-            twice((16, TILE, HD), low),
-            twice((16, TILE, HD), low),
+            twice((16, 2, TILE, HD), low),
             twice((NY * NZ, 2, TILE, HD), low),
             twice((COUNT + 1, 8, HD), full),
             twice((COUNT + 1, 8, HD), full),
+            pltpu.VMEM((3, COUNT, TILE, HD), full),
             twice((NZ, 16, HD), full),
             twice((NZ, 16, HD), full),
             twice((NZ, 16, HD), full),
@@ -569,7 +604,7 @@
             pltpu.SMEM((NY, 1, SLOTS), jnp.int32),
             pltpu.SMEM((9, NY * NZ), jnp.int32),
             dma((9,)), dma((1,)), dma((3, 9)), dma((3, 9)),
-            dma((2, 2, 4, NY)), dma((2, 2, 4, NY)),
+            dma((2, 2, 4, NY)), dma((2, 2, 4, NY)), dma((2, 2, 2)), dma((2, 2, 2)),
             dma((2, NZ - 1)), dma((2, NZ - 1)), dma((2, NZ - 1)), dma((2, NZ - 1)),
             dma((2,)), dma((2, 3)), dma((2, 3)),
             dma((2, 2, 4, NY)), dma((2, 2, 4, NY)),
@@ -584,6 +619,45 @@
     )(rgb, cot, pf, pc, pairs, scale)
 
 
+def finish_kernel(rgb, pose, scale, rgb_out, pose_out, scale_out, rgb_held, pose_held, sem):
+    steps = [
+        (rgb.at[i], rgb_held.at[i], rgb_out.at[i]) for i in range(4)
+    ] + [(pose, pose_held, pose_out)]
+    ins = [
+        pltpu.make_async_copy(src, held, sem.at[0, i]) for i, (src, held, _) in enumerate(steps)
+    ]
+    outs = [
+        pltpu.make_async_copy(held, dst, sem.at[1, i]) for i, (_, held, dst) in enumerate(steps)
+    ]
+    for copy in ins:
+        copy.start()
+    scale_out[...] = scale[0:1, 0:8]
+    for arrive, leave in zip(ins, outs):
+        arrive.wait()
+        leave.start()
+    for copy in outs:
+        copy.wait()
+
+
+def finish(rgb, pose, scale):
+    return pl.pallas_call(
+        finish_kernel,
+        out_shape=(
+            jax.ShapeDtypeStruct(rgb.shape, rgb.dtype),
+            jax.ShapeDtypeStruct(pose.shape, pose.dtype),
+            jax.ShapeDtypeStruct((1, 8), jnp.float32),
+        ),
+        in_specs=[ANY, ANY, VM],
+        out_specs=(ANY, ANY, VM),
+        scratch_shapes=[
+            pltpu.VMEM(rgb.shape, rgb.dtype),
+            pltpu.VMEM(pose.shape, pose.dtype),
+            pltpu.SemaphoreType.DMA((2, 5)),
+        ],
+        compiler_params=pltpu.CompilerParams(vmem_limit_bytes=VMEM_LIMIT),
+    )(rgb, pose, scale)
+
+
 def local(rgb_feat, rgb_grad_out, pose_feat, pose_grad_out, logit_scale, pairs):
     rgb_grad, pose_grad, scale_grad, _ = fused(
         rgb_feat.reshape(4, TILE, 1024),
@@ -593,7 +667,8 @@
         pairs,
         logit_scale,
     )
-    return rgb_grad.reshape(1, 512, 1024), pose_grad[None], scale_grad[0, :8]
+    rgb_grad, pose_grad, scale_grad = finish(rgb_grad, pose_grad, scale_grad)
+    return rgb_grad.reshape(1, 512, 1024), pose_grad[None], scale_grad[0]
 
 
 def solution(mesh):

time: 109 us -> 100 us (0.917); the launches traced: 107 us -> 99.6 us
  local copies, waits for them, and re-layouts: 4.2 us -> 0 us
  Pallas kernels: 102 us -> 98.9 us
    pallas_call x1, Pallas kernels: 102 us -> 95.7 us  [fused(): pl.pallas_call(fused_kernel, out_shape=(jax.ShapeDtypeStruct((4, TILE, 10...]
    pallas_call x0 -> x1, Pallas kernels: none -> 3.27 us  [finish(): pl.pallas_call(finish_kernel, out_shape=(jax.ShapeDtypeStruct(rgb.shape,...]
    unnamed x4 -> x0, local copies, waits for them, and re-layouts: 3.01 us -> none
    squeeze x1 -> x0, local copies, waits for them, and re-layouts: 1.19 us -> none  [local(): return (rgb_grad.reshape(1, 512, 1024), pose_grad[None], scale_grad[0, :8])]
where the time goes in v3:
time: 100 us; the launch traced here: 99.6 us
  Pallas kernels  98.9 us (99%)
    pallas_call x1, Pallas kernels, fused(): pl.pallas_call(fused_kernel, out_shape=(jax.ShapeDtypeStruct((4, TILE, 10...  95.7 us
    pallas_call x1, Pallas kernels, finish(): pl.pallas_call(finish_kernel, out_shape=(jax.ShapeDtypeStruct(rgb.shape,...  3.27 us

profile of v3, /device:TPU:2, one launch (start us, length us, event | category | flops | bytes accessed | tf_op | source)
XLA Modules:
  0.0 99.6 jit_solution(12359240235390735825)
XLA Ops:
  0.6 95.7 %shard_map.85 = (bf16[4,128,1024]{2,1,0:T(8,128)(2,1)}, bf16[128,1024]{1,0:T(8,128)(2,1)}, f32[8,128]{1,0:T(8,128)}, s32[4,1,5]{2,1,0:T(1,128)}) custom-call(bf16[4,128,1024]{2,1,0:T(8,128)(2,1)} %bitcast.7, bf16[4,128,1024]{2,1,0:T(8,128)(2,1)} %bitcast.8, bf16[128,1024]{1,0:T(8,128)(2,1)} %bitcast.9, bf16[128,1024]{1,0:T(8,128)(2,1)} %bitcast.10, ...), custom_call_target="tpu_custom_call" | custom-call | tf_op jit(solution)/shard_map/pallas_call | solution.py:574
  96.3 3.3 %shard_map.86 = (bf16[4,128,1024]{2,1,0:T(8,128)(2,1)}, bf16[128,1024]{1,0:T(8,128)(2,1)}, f32[1,8]{1,0:T(1,128)}) custom-call(bf16[4,128,1024]{2,1,0:T(8,128)(2,1)} %get-tuple-element.9.rgb, bf16[128,1024]{1,0:T(8,128)(2,1)} %get-tuple-element.10.pose, f32[8,128]{1,0:T(8,128)} %get-tuple-element.11.scale), custom_call_target="tpu_custom_call" | custom-call | tf_op jit(solution)/shard_map/pallas_call | solution.py:643

commit v4 on v3

--- a/solution.py
+++ b/solution.py
@@ -15,13 +15,13 @@
 HD = 128
 SLOTS = 5
 COUNT = NY * SLOTS
-VMEM_LIMIT = 56 * 1024 * 1024
+VMEM_LIMIT = 28 * 1024 * 1024
 MESH = pl.DeviceIdType.MESH
 ANY = pl.BlockSpec(memory_space=pl.ANY)
+HBM = pl.BlockSpec(memory_space=pltpu.HBM)
 VM = pl.BlockSpec(memory_space=pltpu.VMEM)
 SM = pl.BlockSpec(memory_space=pltpu.SMEM)
 POSE, RGB, POSE_KEY, RGB_KEY, POSE_PREV, RGB_PREV, RGB_LAST, POSE_END, RGB_END = range(9)
-ORDER = (1, 2, 3, 0)
 CHUNKS = (0, 1, 3, 2)
 STATS_UNROLL = 10
 UNROLL = 5
@@ -201,10 +201,10 @@
     rgb_ref, cot_ref, pf_ref, pc_ref, pairs_ref, scale,
     rgb_grad, pose_grad, scale_out, pairs_x,
     qg, pose, st, rs, keep, ex, got, fin, racc, pacc, sacc,
-    rgbs, rbuf, sbuf, fbuf, sc, s_z, s_y, s_t, codes, tab,
+    rgbs, rbuf, sbuf, fbuf, land, sc, s_z, s_y, s_t, codes, tab,
     own_sem, codes_sem, y_send, y_recv, z_send, z_recv, b_send, b_recv,
     e1_send, e1_recv, e2_send, e2_recv,
-    o_own, o_send, o_recv, r_send, r_recv, f_own, f_send, f_recv,
+    o_own, o_send, o_recv, r_send, r_recv, l_send, l_recv,
     sz_send, sz_recv, sy_send, sy_recv, st_send, st_recv,
 ):
     y, z = place()
@@ -286,7 +286,7 @@
 
     factor = [scale[2 * y + h] / math.sqrt(HD) for h in range(2)]
 
-    def stats(h):
+    def stats(h, low, high):
         def body(m, carry):
             slots = [STATS_UNROLL * m + u for u in range(STATS_UNROLL)]
             news = [slot_stats(n, tab, factor[h], qg[h], pose[h]) for n in slots]
@@ -295,7 +295,7 @@
                 merge(rs[h], n, tab[RGB_PREV, n], *rgb_new)
             return carry
 
-        lax.fori_loop(0, COUNT // STATS_UNROLL, body, 0)
+        lax.fori_loop(low, high, body, 0)
 
     def before(h, low, high):
         def body(m, carry):
@@ -384,41 +384,58 @@
 
     def back(h, side, step, c):
         to = (z + 1) % NZ if side == 0 else (z + NZ - 1) % NZ
+        if step == 3:
+            return remote(
+                sbuf[h].at[side, step, c], land[h].at[side, c],
+                l_send.at[h, side, c], l_recv.at[h, side, c], (y + c) % NY, to,
+            )
         return remote(
             sbuf[h].at[side, step, c], rbuf[h].at[side, step, c],
             r_send.at[h, side, step, c], r_recv.at[h, side, step, c], y, to,
         )
 
+    def straight(h, c):
+        return remote(
+            fbuf[h].at[c], land[h].at[2, c], l_send.at[h, 2, c], l_recv.at[h, 2, c],
+            (y + c) % NY, z,
+        )
+
     def mine(h, block, c):
         return pacc[h][tab[POSE_END, block * NY + (y + c) % NY]]
 
-    def back_step(h, step):
-        for c in ORDER:
-            for side in range(2):
-                if step == 0 and not last_used(side, c):
-                    continue
-                value = mine(h, goal(side, step), c)
-                if step > 1 or (step == 1 and last_used(side, c)):
-                    back(h, side, step - 1, c).wait_recv()
-                    value = value + rbuf[h][side, step - 1, c].astype(jnp.float32)
-                sbuf[h][side, step, c] = value.astype(jnp.bfloat16)
-                start(back(h, side, step, c))
-
-    def final(h, c):
-        src = fbuf[h].at[c]
-        dst = pose_grad.at[:, columns(y, h)]
-        if c == 0:
-            return pltpu.make_async_copy(src, dst, f_own.at[h])
-        return remote(src, dst, f_send.at[h, c - 1], f_recv.at[h, c - 1], (y + c) % NY, z)
+    def back_one(h, side, step, c):
+        value = mine(h, goal(side, step), c)
+        if step > 1 or (step == 1 and last_used(side, c)):
+            back(h, side, step - 1, c).wait_recv()
+            value = value + rbuf[h][side, step - 1, c].astype(jnp.float32)
+        sbuf[h][side, step, c] = value.astype(jnp.bfloat16)
+        start(back(h, side, step, c))
+
+    def back_step(h, phase):
+        for late in range(2):
+            step = phase + late
+            if step > 3:
+                continue
+            for i in range(2):
+                for side in range(2):
+                    c = i + 2 * ((side + late) % 2)
+                    back_one(h, side, step, c)
+        if phase == 0:
+            for c in range(1, NY):
+                fbuf[h][c] = mine(h, z, c).astype(jnp.bfloat16)
+                start(straight(h, c))
 
     def back_end(h):
-        for c in ORDER:
-            value = mine(h, z, c)
+        for c in (2, 3, 1, 0):
+            if c == 0:
+                value = mine(h, z, c)
+            else:
+                straight(h, c).wait_recv()
+                value = land[h][2, c].astype(jnp.float32)
             for side in range(2):
                 back(h, side, 3, c).wait_recv()
-                value = value + rbuf[h][side, 3, c].astype(jnp.float32)
-            fbuf[h][c] = value.astype(jnp.bfloat16)
-            final(h, c).start()
+                value = value + land[h][side, c].astype(jnp.float32)
+            pose_grad[:, columns((y + NY - c) % NY, h)] = value.astype(jnp.bfloat16)
 
     def z_scale(k):
         return remote(sc, s_z.at[z], sz_send.at[k - 1], sz_recv.at[k - 1], y, (z + k) % NZ)
@@ -469,7 +486,9 @@
         scale_out[...] = total_of(s_t, NT)
 
     greet(
-        [((y + k) % NY, z) for k in range(1, NY)] + [(y, (z + k) % NZ) for k in range(1, NZ)],
+        [((y + k) % NY, z) for k in range(1, NY)]
+        + [(y, (z + k) % NZ) for k in range(1, NZ)]
+        + [((y + k) % NY, (z + side) % NZ) for k in range(1, NY) for side in (1, NZ - 1)],
         [(t + k) % NT for k in range(1, NT)],
     )
     for h in range(2):
@@ -493,7 +512,7 @@
         sacc[h] = jnp.zeros((8, HD), jnp.float32)
     for c in CHUNKS[1:]:
         ring(0, 0, c)
-    for i in (3, 4, 7, 8):
+    for i in (3, 4):
         for k in (1, 2, 3):
             start(across(k, i))
         own(i).start()
@@ -509,22 +528,29 @@
     ring_all(0, 3)
     for c in CHUNKS[1:]:
         ring(1, 0, c)
+    for i in (7, 8):
+        for k in (1, 2, 3):
+            start(across(k, i))
+        own(i).start()
     ring_end(0)
-    ring_all(1, 1)
     rgb_arrived(0)
-    stats(0)
+    ring(1, 1, CHUNKS[0])
+    stats(0, 0, 1)
+    ring(1, 1, CHUNKS[1])
+    stats(0, 1, 2)
+    ring(1, 1, CHUNKS[2])
     ex_first(0)
+    ring(1, 1, CHUNKS[3])
+    before(0, 0, 1)
     ring(1, 2, CHUNKS[0])
+    before(0, 1, 2)
     ring(1, 2, CHUNKS[1])
-    before(0, 0, 1)
+    before(0, 2, 3)
     ring(1, 2, CHUNKS[2])
-    before(0, 1, 2)
+    ex_second(0)
     ring(1, 2, CHUNKS[3])
-    before(0, 2, 3)
-    ex_second(0)
-    ring(1, 3, CHUNKS[0])
     before(0, 3, 4)
-    for c in CHUNKS[1:]:
+    for c in CHUNKS:
         ring(1, 3, c)
     ex_end(0)
     after(0, 0, 4)
@@ -533,7 +559,7 @@
         rgb_send(0, pos)
     ring_end(1)
     rgb_arrived(1)
-    stats(1)
+    stats(1, 0, 2)
     ex_first(1)
     back_step(0, 1)
     before(1, 0, 2)
@@ -544,12 +570,12 @@
     ex_end(1)
     after(1, 0, 4)
     back_step(1, 0)
+    scale_first()
     for pos in range(4):
         rgb_send(1, pos)
-    scale_first()
-    back_end(0)
     back_step(1, 1)
     scale_second()
+    back_end(0)
     back_step(1, 2)
     scale_third()
     back_step(1, 3)
@@ -558,8 +584,6 @@
     for h in range(2):
         for pos in range(4):
             rgb_copy(h, pos).wait()
-        for c in range(NY):
-            final(h, c).wait()
     for copy in sent:
         copy.wait_send()
 
@@ -579,8 +603,8 @@
             jax.ShapeDtypeStruct((8, HD), full),
             jax.ShapeDtypeStruct((NY, 1, SLOTS), jnp.int32),
         ),
-        in_specs=[ANY] * 5 + [SM],
-        out_specs=(ANY, ANY, VM, ANY),
+        in_specs=[HBM] * 5 + [SM],
+        out_specs=(VM, VM, VM, HBM),
         scratch_shapes=[
             twice((16, 2, TILE, HD), low),
             twice((NY * NZ, 2, TILE, HD), low),
@@ -594,9 +618,10 @@
             twice((COUNT + 1, TILE, HD), full),
             pltpu.VMEM((2, 8, HD), full),
             twice((4, 4, TILE, HD), low),
-            twice((2, 4, NY, TILE, HD), low),
+            twice((2, 3, NY, TILE, HD), low),
             twice((2, 4, NY, TILE, HD), low),
             twice((NY, TILE, HD), low),
+            twice((3, NY, TILE, HD), low),
             pltpu.VMEM((8, HD), full),
             pltpu.VMEM((NZ, 8, HD), full),
             pltpu.VMEM((NY, 8, HD), full),
@@ -607,8 +632,8 @@
             dma((2, 2, 4, NY)), dma((2, 2, 4, NY)), dma((2, 2, 2)), dma((2, 2, 2)),
             dma((2, NZ - 1)), dma((2, NZ - 1)), dma((2, NZ - 1)), dma((2, NZ - 1)),
             dma((2,)), dma((2, 3)), dma((2, 3)),
-            dma((2, 2, 4, NY)), dma((2, 2, 4, NY)),
-            dma((2,)), dma((2, 3)), dma((2, 3)),
+            dma((2, 2, 3, NY)), dma((2, 2, 3, NY)),
+            dma((2, 3, NY)), dma((2, 3, NY)),
             dma((NZ - 1,)), dma((NZ - 1,)),
             dma((NY - 1,)), dma((NY - 1,)),
             dma((NT - 1,)), dma((NT - 1,)),
@@ -619,23 +644,14 @@
     )(rgb, cot, pf, pc, pairs, scale)
 
 
-def finish_kernel(rgb, pose, scale, rgb_out, pose_out, scale_out, rgb_held, pose_held, sem):
-    steps = [
-        (rgb.at[i], rgb_held.at[i], rgb_out.at[i]) for i in range(4)
-    ] + [(pose, pose_held, pose_out)]
-    ins = [
-        pltpu.make_async_copy(src, held, sem.at[0, i]) for i, (src, held, _) in enumerate(steps)
-    ]
-    outs = [
-        pltpu.make_async_copy(held, dst, sem.at[1, i]) for i, (_, held, dst) in enumerate(steps)
-    ]
-    for copy in ins:
+def finish_kernel(rgb, pose, scale, rgb_out, pose_out, scale_out, sem):
+    copies = [
+        pltpu.make_async_copy(rgb.at[i], rgb_out.at[i], sem.at[i]) for i in range(4)
+    ] + [pltpu.make_async_copy(pose, pose_out, sem.at[4])]
+    for copy in copies:
         copy.start()
     scale_out[...] = scale[0:1, 0:8]
-    for arrive, leave in zip(ins, outs):
-        arrive.wait()
-        leave.start()
-    for copy in outs:
+    for copy in copies:
         copy.wait()
 
 
@@ -647,25 +663,26 @@
             jax.ShapeDtypeStruct(pose.shape, pose.dtype),
             jax.ShapeDtypeStruct((1, 8), jnp.float32),
         ),
-        in_specs=[ANY, ANY, VM],
-        out_specs=(ANY, ANY, VM),
-        scratch_shapes=[
-            pltpu.VMEM(rgb.shape, rgb.dtype),
-            pltpu.VMEM(pose.shape, pose.dtype),
-            pltpu.SemaphoreType.DMA((2, 5)),
-        ],
+        in_specs=[VM, VM, VM],
+        out_specs=(HBM, HBM, VM),
+        scratch_shapes=[pltpu.SemaphoreType.DMA((5,))],
         compiler_params=pltpu.CompilerParams(vmem_limit_bytes=VMEM_LIMIT),
     )(rgb, pose, scale)
 
 
 def local(rgb_feat, rgb_grad_out, pose_feat, pose_grad_out, logit_scale, pairs):
     rgb_grad, pose_grad, scale_grad, _ = fused(
-        rgb_feat.reshape(4, TILE, 1024),
-        rgb_grad_out.reshape(4, TILE, 1024),
-        pose_feat[0],
-        pose_grad_out[0],
-        pairs,
-        logit_scale,
+        *(
+            pltpu.with_memory_space_constraint(part, pltpu.HBM)
+            for part in (
+                rgb_feat.reshape(4, TILE, 1024),
+                rgb_grad_out.reshape(4, TILE, 1024),
+                pose_feat[0],
+                pose_grad_out[0],
+                pairs,
+            )
+        ),
+        pltpu.with_memory_space_constraint(logit_scale, pltpu.HBM),
     )
     rgb_grad, pose_grad, scale_grad = finish(rgb_grad, pose_grad, scale_grad)
     return rgb_grad.reshape(1, 512, 1024), pose_grad[None], scale_grad[0]

time: 100 us -> 96.8 us (0.968)
  Pallas kernels: 98.9 us -> 94.8 us
    pallas_call x1, Pallas kernels: 95.7 us -> 93.2 us  [fused(): pl.pallas_call(fused_kernel, out_shape=(jax.ShapeDtypeStruct((4, TILE, 10...]
    pallas_call x1, Pallas kernels: 3.27 us -> 1.6 us  [finish(): pl.pallas_call(finish_kernel, out_shape=(jax.ShapeDtypeStruct(rgb.shape,...]
where the time goes in v4:
time: 96.8 us; the launch traced here: 95.4 us
  Pallas kernels  94.8 us (98%)
    pallas_call x1, Pallas kernels, fused(): pl.pallas_call(fused_kernel, out_shape=(jax.ShapeDtypeStruct((4, TILE, 10...  93.2 us

profile of v4, /device:TPU:2, one launch (start us, length us, event | category | flops | bytes accessed | tf_op | source)
XLA Modules:
  0.0 95.4 jit_solution(9286902107200852377)
XLA Ops:
  0.6 93.2 %shard_map.85 = (bf16[4,128,1024]{2,1,0:T(8,128)(2,1)S(1)}, bf16[128,1024]{1,0:T(8,128)(2,1)S(1)}, f32[8,128]{1,0:T(8,128)S(1)}, s32[4,1,5]{2,1,0:T(1,128)}) custom-call(bf16[4,128,1024]{2,1,0:T(8,128)(2,1)} %bitcast.7, bf16[4,128,1024]{2,1,0:T(8,128)(2,1)} %bitcast.8, bf16[128,1024]{1,0:T(8,128)(2,1)} %bitcast.9, bf16[128,1024]{1,0:T(8,128)(2,1)} %bitcast.10, ...), custom_call_target="tpu_custom_call" | custom-call | tf_op jit(solution)/shard_map/pallas_call | solution.py:598
  93.8 1.6 %shard_map.86 = (bf16[4,128,1024]{2,1,0:T(8,128)(2,1)}, bf16[128,1024]{1,0:T(8,128)(2,1)}, f32[1,8]{1,0:T(1,128)}) custom-call(bf16[4,128,1024]{2,1,0:T(8,128)(2,1)S(1)} %get-tuple-element.9.rgb, bf16[128,1024]{1,0:T(8,128)(2,1)S(1)} %get-tuple-element.10.pose, f32[8,128]{1,0:T(8,128)S(1)} %get-tuple-element.11.scale), custom_call_target="tpu_custom_call" | custom-call | tf_op jit(solution)/shard_map/pallas_call | solution.py:659

commit v5 on v4

--- a/solution.py
+++ b/solution.py
@@ -23,6 +23,7 @@
 SM = pl.BlockSpec(memory_space=pltpu.SMEM)
 POSE, RGB, POSE_KEY, RGB_KEY, POSE_PREV, RGB_PREV, RGB_LAST, POSE_END, RGB_END = range(9)
 CHUNKS = (0, 1, 3, 2)
+FAR = (4, 3, 5, 2, 6, 1, 7)
 STATS_UNROLL = 10
 UNROLL = 5
 
@@ -332,16 +333,16 @@
         return remote(ref, ref, e2_send.at[h, k - 1], e2_recv.at[h, k - 1], y, (z + k) % NZ)
 
     def ex_first(h):
-        def pack(zz, carry):
+        def pack(zz):
             for yy in range(NY):
                 last = tab[POSE_END, zz * NY + yy]
                 for i in range(3):
                     ex[h][zz, 4 * i + yy:4 * i + yy + 1, :] = st[h][last, i:i + 1, :]
-            return carry
-
-        lax.fori_loop(0, NZ, pack, 0)
-        for k in range(1, NZ):
+
+        for k in FAR:
+            pack((z + k) % NZ)
             start(ex_copy(h, k))
+        pack(z)
         got[h][z] = ex[h][z]
 
     def ex_second(h):
@@ -360,7 +361,7 @@
         fin[h][z, 0:4, :] = top
         fin[h][z, 4:8, :] = inverse
         fin[h][z, 8:12, :] = inner * inverse
-        for k in range(1, NZ):
+        for k in FAR:
             start(fin_copy(h, k))
 
     def ex_end(h):
@@ -462,7 +463,7 @@
             part = jnp.sum(part, axis=1, keepdims=True) / scale[2 * y + h]
             tile = jnp.where(lane == 2 * y + h, part, tile)
         sc[...] = tile
-        for k in range(1, NZ):
+        for k in FAR:
             start(z_scale(k))
         s_z[z] = tile
 

time: 96.8 us -> 95.7 us (0.989); the launches traced: 95.4 us -> 95.3 us
  no operation moved by 1% of the time
where the time goes in v5:
time: 95.7 us; the launch traced here: 95.3 us
  Pallas kernels  94.7 us (99%)
    pallas_call x1, Pallas kernels, fused(): pl.pallas_call(fused_kernel, out_shape=(jax.ShapeDtypeStruct((4, TILE, 10...  93.1 us

profile of v5, /device:TPU:2, one launch (start us, length us, event | category | flops | bytes accessed | tf_op | source)
XLA Modules:
  0.0 95.3 jit_solution(5981635975776135604)
XLA Ops:
  0.6 93.1 %shard_map.85 = (bf16[4,128,1024]{2,1,0:T(8,128)(2,1)S(1)}, bf16[128,1024]{1,0:T(8,128)(2,1)S(1)}, f32[8,128]{1,0:T(8,128)S(1)}, s32[4,1,5]{2,1,0:T(1,128)}) custom-call(bf16[4,128,1024]{2,1,0:T(8,128)(2,1)} %bitcast.7, bf16[4,128,1024]{2,1,0:T(8,128)(2,1)} %bitcast.8, bf16[128,1024]{1,0:T(8,128)(2,1)} %bitcast.9, bf16[128,1024]{1,0:T(8,128)(2,1)} %bitcast.10, ...), custom_call_target="tpu_custom_call" | custom-call | tf_op jit(solution)/shard_map/pallas_call | solution.py:599
  93.7 1.6 %shard_map.86 = (bf16[4,128,1024]{2,1,0:T(8,128)(2,1)}, bf16[128,1024]{1,0:T(8,128)(2,1)}, f32[1,8]{1,0:T(1,128)}) custom-call(bf16[4,128,1024]{2,1,0:T(8,128)(2,1)S(1)} %get-tuple-element.9.rgb, bf16[128,1024]{1,0:T(8,128)(2,1)S(1)} %get-tuple-element.10.pose, f32[8,128]{1,0:T(8,128)S(1)} %get-tuple-element.11.scale), custom_call_target="tpu_custom_call" | custom-call | tf_op jit(solution)/shard_map/pallas_call | solution.py:660

commit v6 on v5

--- a/solution.py
+++ b/solution.py
@@ -24,6 +24,7 @@
 POSE, RGB, POSE_KEY, RGB_KEY, POSE_PREV, RGB_PREV, RGB_LAST, POSE_END, RGB_END = range(9)
 CHUNKS = (0, 1, 3, 2)
 FAR = (4, 3, 5, 2, 6, 1, 7)
+ACROSS = (2, 1, 3)
 STATS_UNROLL = 10
 UNROLL = 5
 
@@ -471,14 +472,14 @@
         for k in range(1, NZ):
             z_scale(k).wait_recv()
         s_y[y] = total_of(s_z, NZ)
-        for k in range(1, NY):
+        for k in ACROSS:
             start(y_scale(k))
 
     def scale_third():
         for k in range(1, NY):
             y_scale(k).wait_recv()
         s_t[t] = total_of(s_y, NY)
-        for k in range(1, NT):
+        for k in FAR:
             start(t_scale(k))
 
     def scale_end():
@@ -487,17 +488,17 @@
         scale_out[...] = total_of(s_t, NT)
 
     greet(
-        [((y + k) % NY, z) for k in range(1, NY)]
-        + [(y, (z + k) % NZ) for k in range(1, NZ)]
-        + [((y + k) % NY, (z + side) % NZ) for k in range(1, NY) for side in (1, NZ - 1)],
-        [(t + k) % NT for k in range(1, NT)],
+        [(y, (z + k) % NZ) for k in FAR]
+        + [((y + k) % NY, (z + side) % NZ) for k in ACROSS for side in (1, NZ - 1)]
+        + [((y + k) % NY, z) for k in ACROSS],
+        [(t + k) % NT for k in FAR],
     )
     for h in range(2):
         for i in range(2):
             for side in range(2):
                 start(begin(h, side, i))
         for i in (1 + 4 * h, 2 + 4 * h):
-            for k in (1, 2, 3):
+            for k in ACROSS:
                 start(across(k, i))
     for k in (1, 2, 3):
         start(across(k, 0))
@@ -514,7 +515,7 @@
     for c in CHUNKS[1:]:
         ring(0, 0, c)
     for i in (3, 4):
-        for k in (1, 2, 3):
+        for k in ACROSS:
             start(across(k, i))
         own(i).start()
     for k in (1, 2, 3):
@@ -530,7 +531,7 @@
     for c in CHUNKS[1:]:
         ring(1, 0, c)
     for i in (7, 8):
-        for k in (1, 2, 3):
+        for k in ACROSS:
             start(across(k, i))
         own(i).start()
     ring_end(0)

time: 95.7 us -> 95.7 us (level)
  no operation moved by 1% of the time
where the time goes in v6:
time: 95.7 us; the launch traced here: 95.4 us
  Pallas kernels  94.7 us (99%)
    pallas_call x1, Pallas kernels, fused(): pl.pallas_call(fused_kernel, out_shape=(jax.ShapeDtypeStruct((4, TILE, 10...  93.1 us

profile of v6, /device:TPU:2, one launch (start us, length us, event | category | flops | bytes accessed | tf_op | source)
XLA Modules:
  0.0 95.4 jit_solution(12105461324052005157)
XLA Ops:
  0.6 93.1 %shard_map.85 = (bf16[4,128,1024]{2,1,0:T(8,128)(2,1)S(1)}, bf16[128,1024]{1,0:T(8,128)(2,1)S(1)}, f32[8,128]{1,0:T(8,128)S(1)}, s32[4,1,5]{2,1,0:T(1,128)}) custom-call(bf16[4,128,1024]{2,1,0:T(8,128)(2,1)} %bitcast.7, bf16[4,128,1024]{2,1,0:T(8,128)(2,1)} %bitcast.8, bf16[128,1024]{1,0:T(8,128)(2,1)} %bitcast.9, bf16[128,1024]{1,0:T(8,128)(2,1)} %bitcast.10, ...), custom_call_target="tpu_custom_call" | custom-call | tf_op jit(solution)/shard_map/pallas_call | solution.py:600
  93.7 1.6 %shard_map.86 = (bf16[4,128,1024]{2,1,0:T(8,128)(2,1)}, bf16[128,1024]{1,0:T(8,128)(2,1)}, f32[1,8]{1,0:T(1,128)}) custom-call(bf16[4,128,1024]{2,1,0:T(8,128)(2,1)S(1)} %get-tuple-element.9.rgb, bf16[128,1024]{1,0:T(8,128)(2,1)S(1)} %get-tuple-element.10.pose, f32[8,128]{1,0:T(8,128)S(1)} %get-tuple-element.11.scale), custom_call_target="tpu_custom_call" | custom-call | tf_op jit(solution)/shard_map/pallas_call | solution.py:661
